TPU v7x, 32 devices: a whole 2x2x4 slice. The times are simulated.
32 devices in a mesh: seq: 4 (over y, x), batch: 8 (over z, core).
Axes of the slice: x: 2, y: 2, z: 4, core: 2. Of those that a mesh axis runs over, the one named last changes fastest.
Arguments:
- inputs: bfloat16 [24, 896, 768], P('batch', 'seq'), may hold values from -6 to 6
- lengths: int32 [24], P('batch'), may hold values from 672 to 896, as said below
- gain_one: bfloat16 [768], replicated, may hold values from 0.5 to 1.5
- shift_one: bfloat16 [768], replicated, may hold values from -1.5 to 1.5
- w_query: bfloat16 [768, 768], replicated, may hold values from -0.4375 to 0.4375
- b_query: bfloat16 [768], replicated, may hold values from -1.5 to 1.5
- w_key: bfloat16 [768, 768], replicated, may hold values from -0.21875 to 0.21875
- w_value: bfloat16 [768, 768], replicated, may hold values from -0.21875 to 0.21875
- b_value: bfloat16 [768], replicated, may hold values from -1.5 to 1.5
- w_out: bfloat16 [768, 768], replicated, may hold values from -0.875 to 0.875
- b_out: bfloat16 [768], replicated, may hold values from -1.5 to 1.5
- gain_two: bfloat16 [768], replicated, may hold values from 0.5 to 1.5
- shift_two: bfloat16 [768], replicated, may hold values from -1.5 to 1.5
- w_up: bfloat16 [768, 3072], replicated, may hold values from -0.21875 to 0.21875
- b_up: bfloat16 [3072], replicated, may hold values from -1.5 to 1.5
- w_down: bfloat16 [3072, 768], replicated, may hold values from -0.109375 to 0.109375
- b_down: bfloat16 [768], replicated, may hold values from -1.5 to 1.5
- cotangent: bfloat16 [24, 896, 768], P('batch', 'seq'), may hold values from -6 to 6
Outputs:
- outputs: bfloat16 [24, 896, 768], P('batch', 'seq')
- input_grad: bfloat16 [24, 896, 768], P('batch', 'seq')
- grad_gain_one: float32 [768], P('batch')
- grad_shift_one: float32 [768], P('batch')
- grad_w_query: float32 [768, 768], P('batch')
- grad_b_query: float32 [768], P('batch')
- grad_w_key: float32 [768, 768], P('batch')
- grad_w_value: float32 [768, 768], P('batch')
- grad_b_value: float32 [768], P('batch')
- grad_w_out: float32 [768, 768], P('batch')
- grad_b_out: float32 [768], P('batch')
- grad_gain_two: float32 [768], P('batch')
- grad_shift_two: float32 [768], P('batch')
- grad_w_up: float32 [768, 3072], P('batch')
- grad_b_up: float32 [3072], P('batch')
- grad_w_down: float32 [3072, 768], P('batch')
- grad_b_down: float32 [768], P('batch')
Inputs may be any that keep to these rules, and one draw needn't show every extreme that they name: Rows 0 to lengths - 1 of a sequence are valid keys; in each aligned block of 3 sequences one has length 896.
All inputs are finite; a program needn't handle non-finite values.
Results may differ from a plain program's by a relative error of at most 0.022.
Values may be sent and summed in bfloat16 or wider, within the bound.
A program may use at most 256 MiB of HBM per device.

v0:
```python
import jax
import jax.numpy as jnp
from jax import lax
from jax.sharding import PartitionSpec as P

HEAD_DIM = 64


norm_eps = 1e-05
masked_score = -1e30


def from_behind(x, axis, by):
    length = lax.axis_size(axis)
    return lax.ppermute(x, axis, [(i, (i + by) % length) for i in range(length)])


def normed(values, gain, offset):
    average = jnp.mean(values, axis=-1, keepdims=True)
    centred = values - average
    spread = jnp.mean(centred * centred, axis=-1, keepdims=True)
    return centred * lax.rsqrt(spread + norm_eps) * gain + offset


def outer_sum(left, right):
    return lax.dot_general(
        left, right, (((0,), (0,)), ((), ())), preferred_element_type=jnp.float32
    )


def back_dot(grad_rows, weight):
    return lax.dot_general(
        grad_rows, weight, (((1,), (1,)), ((), ())), preferred_element_type=jnp.float32
    )


def front_dot(rows_low, weight, bias):
    return jnp.dot(rows_low, weight, preferred_element_type=jnp.float32) + bias.astype(jnp.float32)


def column_sums(values):
    return jnp.sum(values.astype(jnp.float32), axis=0)


def key_valid(lengths, source, block_rows):
    positions = source * block_rows + jnp.arange(block_rows, dtype=jnp.int32)
    return (positions[None, :] < lengths[:, None])[:, None, None, :]


def block_scores(queries, key_block, valid):
    scores = jnp.einsum(
        "srhd,sthd->srht", queries, key_block, preferred_element_type=jnp.float32
    ) * HEAD_DIM ** (-0.5)
    return jnp.where(valid, scores, masked_score)


def body(
    inputs,
    lengths,
    gain_one,
    shift_one,
    w_query,
    b_query,
    w_key,
    w_value,
    b_value,
    w_out,
    b_out,
    gain_two,
    shift_two,
    w_up,
    b_up,
    w_down,
    b_down,
    cotangent,
):
    cycle_size = lax.axis_size("seq")
    position = lax.axis_index("seq")
    count, block_rows, width = inputs.shape
    heads = width // HEAD_DIM
    total_rows = count * block_rows
    split_shape = (count, block_rows, heads, HEAD_DIM)
    scale = HEAD_DIM ** (-0.5)
    rows_in = inputs.astype(jnp.float32).reshape(total_rows, width)
    first_full, norm_one_pull = jax.vjp(
        normed, rows_in, gain_one.astype(jnp.float32), shift_one.astype(jnp.float32)
    )
    first = first_full.astype(jnp.bfloat16)
    queries = front_dot(first, w_query, b_query).astype(jnp.bfloat16).reshape(split_shape)
    key_rows = jnp.dot(first, w_key, preferred_element_type=jnp.float32).astype(jnp.bfloat16)
    value_rows = front_dot(first, w_value, b_value).astype(jnp.bfloat16)
    own_block = jnp.stack((key_rows, value_rows)).reshape((2,) + split_shape)
    running_max = jnp.full((count, block_rows, heads), masked_score, jnp.float32)
    running_total = jnp.zeros((count, block_rows, heads), jnp.float32)
    running_sum = jnp.zeros(split_shape, jnp.float32)
    moving = own_block
    for rotation in range(cycle_size):
        source = (position - rotation) % cycle_size
        valid = key_valid(lengths, source, block_rows)
        scores = block_scores(queries, moving[0], valid)
        new_max = jnp.maximum(running_max, jnp.max(scores, axis=-1))
        decay = jnp.exp(running_max - new_max)
        weights_exp = jnp.where(valid, jnp.exp(scores - new_max[..., None]), 0.0)
        running_total = running_total * decay + jnp.sum(weights_exp, axis=-1)
        running_sum = running_sum * decay[..., None] + jnp.einsum(
            "srht,sthd->srhd",
            weights_exp.astype(jnp.bfloat16),
            moving[1],
            preferred_element_type=jnp.float32,
        )
        running_max = new_max
        if rotation + 1 < cycle_size:
            moving = from_behind(moving, "seq", 1)
    attended = running_sum / running_total[..., None]
    log_total = running_max + jnp.log(running_total)
    attended_low = attended.reshape(total_rows, width).astype(jnp.bfloat16)
    middle = rows_in + front_dot(attended_low, w_out, b_out)
    second_full, norm_two_pull = jax.vjp(
        normed, middle, gain_two.astype(jnp.float32), shift_two.astype(jnp.float32)
    )
    second = second_full.astype(jnp.bfloat16)
    hidden = front_dot(second, w_up, b_up)
    gelu_value, gelu_pull = jax.vjp(jax.nn.gelu, hidden)
    active = gelu_value.astype(jnp.bfloat16)
    outputs = middle + front_dot(active, w_down, b_down)
    grad_rows_out = cotangent.astype(jnp.float32).reshape(total_rows, width)
    grad_ffn = cotangent.reshape(total_rows, width)
    grad_w_down = outer_sum(active, grad_ffn)
    grad_b_down = column_sums(grad_ffn)
    grad_hidden = gelu_pull(back_dot(grad_ffn, w_down))[0].astype(jnp.bfloat16)
    grad_w_up = outer_sum(second, grad_hidden)
    grad_b_up = column_sums(grad_hidden)
    grad_middle_part, grad_gain_two, grad_shift_two = norm_two_pull(back_dot(grad_hidden, w_up))
    grad_middle = grad_rows_out + grad_middle_part
    grad_branch = grad_middle.astype(jnp.bfloat16)
    grad_w_out = outer_sum(attended_low, grad_branch)
    grad_b_out = column_sums(grad_branch)
    grad_attended = back_dot(grad_branch, w_out).astype(jnp.bfloat16).reshape(split_shape)
    row_delta = jnp.sum(grad_attended.astype(jnp.float32) * attended, axis=-1)
    grad_queries = jnp.zeros(split_shape, jnp.float32)
    carried = jnp.zeros((2,) + split_shape, jnp.float32)
    moving = own_block
    for rotation in range(cycle_size):
        source = (position - rotation) % cycle_size
        valid = key_valid(lengths, source, block_rows)
        scores = block_scores(queries, moving[0], valid)
        probs = jnp.where(valid, jnp.exp(scores - log_total[..., None]), 0.0)
        grad_probs = jnp.einsum(
            "srhd,sthd->srht", grad_attended, moving[1], preferred_element_type=jnp.float32
        )
        grad_scores = (probs * (grad_probs - row_delta[..., None])).astype(jnp.bfloat16)
        grad_queries = (
            grad_queries
            + jnp.einsum(
                "srht,sthd->srhd", grad_scores, moving[0], preferred_element_type=jnp.float32
            )
            * scale
        )
        grad_keys_part = (
            jnp.einsum("srht,srhd->sthd", grad_scores, queries, preferred_element_type=jnp.float32)
            * scale
        )
        grad_values_part = jnp.einsum(
            "srht,srhd->sthd",
            probs.astype(jnp.bfloat16),
            grad_attended,
            preferred_element_type=jnp.float32,
        )
        carried = from_behind(
            (carried + jnp.stack((grad_keys_part, grad_values_part))).astype(jnp.bfloat16), "seq", 1
        ).astype(jnp.float32)
        if rotation + 1 < cycle_size:
            moving = from_behind(moving, "seq", 1)
    grad_keys = carried[0].reshape(total_rows, width).astype(jnp.bfloat16)
    grad_values = carried[1].reshape(total_rows, width).astype(jnp.bfloat16)
    grad_query_rows = grad_queries.reshape(total_rows, width).astype(jnp.bfloat16)
    grad_w_query = outer_sum(first, grad_query_rows)
    grad_b_query = column_sums(grad_query_rows)
    grad_w_key = outer_sum(first, grad_keys)
    grad_w_value = outer_sum(first, grad_values)
    grad_b_value = column_sums(grad_values)
    grad_first = (
        back_dot(grad_query_rows, w_query)
        + back_dot(grad_keys, w_key)
        + back_dot(grad_values, w_value)
    )
    grad_rows_part, grad_gain_one, grad_shift_one = norm_one_pull(grad_first)
    input_grad = grad_middle + grad_rows_part
    scattered = (
        lax.psum_scatter(
            grad_gain_one.astype(jnp.bfloat16), "batch", scatter_dimension=0, tiled=True
        ).astype(jnp.float32),
        lax.psum_scatter(
            grad_shift_one.astype(jnp.bfloat16), "batch", scatter_dimension=0, tiled=True
        ).astype(jnp.float32),
        lax.psum_scatter(
            grad_w_query.astype(jnp.bfloat16), "batch", scatter_dimension=0, tiled=True
        ).astype(jnp.float32),
        lax.psum_scatter(
            grad_b_query.astype(jnp.bfloat16), "batch", scatter_dimension=0, tiled=True
        ).astype(jnp.float32),
        lax.psum_scatter(
            grad_w_key.astype(jnp.bfloat16), "batch", scatter_dimension=0, tiled=True
        ).astype(jnp.float32),
        lax.psum_scatter(
            grad_w_value.astype(jnp.bfloat16), "batch", scatter_dimension=0, tiled=True
        ).astype(jnp.float32),
        lax.psum_scatter(
            grad_b_value.astype(jnp.bfloat16), "batch", scatter_dimension=0, tiled=True
        ).astype(jnp.float32),
        lax.psum_scatter(
            grad_w_out.astype(jnp.bfloat16), "batch", scatter_dimension=0, tiled=True
        ).astype(jnp.float32),
        lax.psum_scatter(
            grad_b_out.astype(jnp.bfloat16), "batch", scatter_dimension=0, tiled=True
        ).astype(jnp.float32),
        lax.psum_scatter(
            grad_gain_two.astype(jnp.bfloat16), "batch", scatter_dimension=0, tiled=True
        ).astype(jnp.float32),
        lax.psum_scatter(
            grad_shift_two.astype(jnp.bfloat16), "batch", scatter_dimension=0, tiled=True
        ).astype(jnp.float32),
        lax.psum_scatter(
            grad_w_up.astype(jnp.bfloat16), "batch", scatter_dimension=0, tiled=True
        ).astype(jnp.float32),
        lax.psum_scatter(
            grad_b_up.astype(jnp.bfloat16), "batch", scatter_dimension=0, tiled=True
        ).astype(jnp.float32),
        lax.psum_scatter(
            grad_w_down.astype(jnp.bfloat16), "batch", scatter_dimension=0, tiled=True
        ).astype(jnp.float32),
        lax.psum_scatter(
            grad_b_down.astype(jnp.bfloat16), "batch", scatter_dimension=0, tiled=True
        ).astype(jnp.float32),
    )
    summed = (
        lax.psum(scattered[0].astype(jnp.bfloat16), "seq").astype(jnp.float32),
        lax.psum(scattered[1].astype(jnp.bfloat16), "seq").astype(jnp.float32),
        lax.psum(scattered[2].astype(jnp.bfloat16), "seq").astype(jnp.float32),
        lax.psum(scattered[3].astype(jnp.bfloat16), "seq").astype(jnp.float32),
        lax.psum(scattered[4].astype(jnp.bfloat16), "seq").astype(jnp.float32),
        lax.psum(scattered[5].astype(jnp.bfloat16), "seq").astype(jnp.float32),
        lax.psum(scattered[6].astype(jnp.bfloat16), "seq").astype(jnp.float32),
        lax.psum(scattered[7].astype(jnp.bfloat16), "seq").astype(jnp.float32),
        lax.psum(scattered[8].astype(jnp.bfloat16), "seq").astype(jnp.float32),
        lax.psum(scattered[9].astype(jnp.bfloat16), "seq").astype(jnp.float32),
        lax.psum(scattered[10].astype(jnp.bfloat16), "seq").astype(jnp.float32),
        lax.psum(scattered[11].astype(jnp.bfloat16), "seq").astype(jnp.float32),
        lax.psum(scattered[12].astype(jnp.bfloat16), "seq").astype(jnp.float32),
        lax.psum(scattered[13].astype(jnp.bfloat16), "seq").astype(jnp.float32),
        lax.psum(scattered[14].astype(jnp.bfloat16), "seq").astype(jnp.float32),
    )
    return (
        outputs.astype(jnp.bfloat16).reshape(inputs.shape),
        input_grad.astype(jnp.bfloat16).reshape(inputs.shape),
        summed[0],
        summed[1],
        summed[2],
        summed[3],
        summed[4],
        summed[5],
        summed[6],
        summed[7],
        summed[8],
        summed[9],
        summed[10],
        summed[11],
        summed[12],
        summed[13],
        summed[14],
    )


def solution(mesh):
    placed = (
        P("batch", "seq", None),
        P("batch"),
        P(),
        P(),
        P(),
        P(),
        P(),
        P(),
        P(),
        P(),
        P(),
        P(),
        P(),
        P(),
        P(),
        P(),
        P(),
        P("batch", "seq", None),
    )
    return jax.shard_map(
        body,
        mesh=mesh,
        in_specs=placed,
        out_specs=(
            P("batch", "seq", None),
            P("batch", "seq", None),
            P("batch"),
            P("batch"),
            P("batch", None),
            P("batch"),
            P("batch", None),
            P("batch", None),
            P("batch"),
            P("batch", None),
            P("batch"),
            P("batch"),
            P("batch"),
            P("batch", None),
            P("batch"),
            P("batch", None),
            P("batch"),
        ),
        check_vma=False,
    )
```

profile of v0, /device:TPU:0, one launch (start us, length us, event | category | flops | bytes accessed | tf_op | source)
XLA Modules:
  0.0 718.6 jit_solution(13532472256681963358)
XLA Ops:
  41.0 52.3 %collective-permute-done = bf16[2,3,224,12,64]{2,4,3,1,0:T(8,128)(2,1)} collective-permute-done((bf16[2,3,224,12,64]{2,4,3,1,0:T(8,128)(2,1)S(1)}, bf16[2,3,224,12,64]{2,4,3,1,0:T(8,128)(2,1)}, u32[]{:S(2)}, u32[]{:S(2)}) %collective-permute-start) | collective-permute-done | bytes 2064416 | tf_op jit(solution)/shard_map/ppermute | solution.py:15
  119.3 27.6 %collective-permute-done.1 = bf16[2,3,224,12,64]{2,4,3,1,0:T(8,128)(2,1)} collective-permute-done((bf16[2,3,224,12,64]{2,4,3,1,0:T(8,128)(2,1)}, bf16[2,3,224,12,64]{2,4,3,1,0:T(8,128)(2,1)}, u32[]{:S(2)}, u32[]{:S(2)}) %collective-permute-start.1) | collective-permute-done | bytes 2064416 | tf_op jit(solution)/shard_map/ppermute | solution.py:15
  148.7 5.2 bitcast_reduce_fusion.3
  161.4 38.3 %collective-permute-done.2 = bf16[2,3,224,12,64]{2,4,3,1,0:T(8,128)(2,1)S(1)} collective-permute-done((bf16[2,3,224,12,64]{2,4,3,1,0:T(8,128)(2,1)}, bf16[2,3,224,12,64]{2,4,3,1,0:T(8,128)(2,1)S(1)}, u32[]{:S(2)}, u32[]{:S(2)}) %collective-permute-start.2) | collective-permute-done | bytes 2064416 | tf_op jit(solution)/shard_map/ppermute | solution.py:15
  201.9 8.3 %fusion.58 = f32[3,12,64,224]{3,2,1,0:T(8,128)S(1)} fusion(bf16[3,224,12,64]{1,3,2,0:T(8,128)(2,1)S(1)} %copy-done.30, f32[3,12,224,224]{3,2,1,0:T(8,128)} %get-tuple-element.79, f32[3,224,12]{1,2,0:T(8,128)S(1)} %get-tuple-element.65, pred[3,224]{1,0:T(4,128)(4,1)S(1)} %get-tuple-element.68), kind=kOutput, calls=%fused_computation.80 | convolution fusion | flops 240242688 | bytes 10354848 | tf_op jit(solution)/shard_map/srht,sthd->srhd/dot_general | solution.py:105
  210.1 7.0 fusion.32
  243.6 5.9 fusion.134
  249.6 8.5 %fusion.135 = (bf16[3072]{0:T(1024)(128)(2,1)S(1)}, bf16[672,3072]{1,0:T(8,128)(2,1)S(1)}) fusion(f32[672,3072]{1,0:T(8,128)S(1)} %fusion.134, f32[3072]{0:T(1024)S(1)} %convert_element_type.295, bf16[672,768]{1,0:T(8,128)(2,1)S(1)} %bitcast.309, bf16[3072,768]{1,0:T(8,128)(2,1)S(1)} %bitcast.318), kind=kOutput, calls=%fused_computation.211 | convolution fusion | flops 3216307200 | bytes 18155520 | tf_op jit(solution)/shard_map/dot_general | solution.py:32
  282.7 6.7 fusion.14
  298.7 6.7 fusion.12
  329.7 10.8 %convolution_convert_fusion = bf16[3072,768]{1,0:T(8,128)(2,1)} fusion(bf16[672,768]{1,0:T(8,128)(2,1)S(1)} %bitcast.310, f32[672,3072]{1,0:T(8,128)} %copy-done.52, f32[3072]{0:T(1024)S(1)} %convert_element_type.295), kind=kOutput, calls=%fused_computation.66 | convolution fusion | flops 3193896960 | bytes 14020608 | tf_op jit(solution)/shard_map/dot_general | solution.py:26
  344.3 5.7 fusion.97
  352.0 6.3 convolution_convert_fusion.1
  362.1 5.7 fusion.82
  367.8 36.1 %collective-permute-done.3 = bf16[2,3,224,12,64]{2,4,3,1,0:T(8,128)(2,1)} collective-permute-done((bf16[2,3,224,12,64]{2,4,3,1,0:T(8,128)(2,1)}, bf16[2,3,224,12,64]{2,4,3,1,0:T(8,128)(2,1)}, u32[]{:S(2)}, u32[]{:S(2)}) %collective-permute-start.3) | collective-permute-done | bytes 2064416 | tf_op jit(solution)/shard_map/ppermute | solution.py:15
  410.9 46.5 %collective-permute-done.4 = bf16[2,3,224,12,64]{2,4,3,1,0:T(8,128)(2,1)S(1)} collective-permute-done((bf16[2,3,224,12,64]{2,4,3,1,0:T(8,128)(2,1)S(1)}, bf16[2,3,224,12,64]{2,4,3,1,0:T(8,128)(2,1)S(1)}, u32[]{:S(2)}, u32[]{:S(2)}) %collective-permute-start.4) | collective-permute-done | bytes 2064416 | tf_op jit(solution)/shard_map/ppermute | solution.py:15
  463.7 45.1 %collective-permute-done.5 = bf16[2,3,224,12,64]{2,4,3,1,0:T(8,128)(2,1)S(1)} collective-permute-done((bf16[2,3,224,12,64]{2,4,3,1,0:T(8,128)(2,1)S(1)}, bf16[2,3,224,12,64]{2,4,3,1,0:T(8,128)(2,1)S(1)}, u32[]{:S(2)}, u32[]{:S(2)}) %collective-permute-start.5) | collective-permute-done | bytes 2064416 | tf_op jit(solution)/shard_map/ppermute | solution.py:15
  509.9 49.0 %collective-permute-done.6 = bf16[2,3,224,12,64]{2,4,3,1,0:T(8,128)(2,1)S(1)} collective-permute-done((bf16[2,3,224,12,64]{2,4,3,1,0:T(8,128)(2,1)S(1)}, bf16[2,3,224,12,64]{2,4,3,1,0:T(8,128)(2,1)S(1)}, u32[]{:S(2)}, u32[]{:S(2)}) %collective-permute-start.6) | collective-permute-done | bytes 2064416 | tf_op jit(solution)/shard_map/ppermute | solution.py:15
  586.7 10.9 %add_convert_fusion.2 = bf16[672,768]{1,0:T(8,128)(2,1)} fusion(f32[672,768]{1,0:T(8,128)S(1)} %copy-done.21, bf16[3072,768]{1,0:T(8,128)(2,1)} %param.33, f32[768]{0:T(1024)S(1)} %convert_element_type.297, f32[672,3072]{1,0:T(8,128)} %copy-done.52, f32[3072]{0:T(1024)S(1)} %convert_element_type.295), kind=kOutput, calls=%fused_computation.126 | convolution fusion | flops 3193085952 | bytes 16088064 | tf_op jit(solution)/shard_map/dot_general | solution.py:38
  602.0 32.0 %reduce-scatter.9.cloned.1.call-done = bf16[96,768]{1,0:T(8,128)(2,1)} async-done(((bf16[768,768]{1,0:T(8,128)(2,1)}), bf16[96,768]{1,0:T(8,128)(2,1)}) %reduce-scatter.9.cloned.1.call-update) | async-done | bytes 147472 | tf_op jit(solution)/shard_map/reduce_scatter | solution.py:202
  634.1 5.0 multiply_reduce_fusion.2
  639.1 26.0 %all-reduce.9 = (bf16[768]{0:T(1024)(128)(2,1)S(1)}, bf16[768]{0:T(1024)(128)(2,1)S(1)}, bf16[768]{0:T(1024)(128)(2,1)S(1)}, bf16[768]{0:T(1024)(128)(2,1)S(1)},...) all-reduce(bf16[768]{0:T(1024)(128)(2,1)S(1)} %get-tuple-element.19, ...), channel_id=2, replica_groups=mesh['seq'=4,'batch'=8] {'batch'}, use_global_device_ids=true, to_apply=%region_18.19.clone | all-reduce | flops 9216 | bytes 36864
  665.9 10.1 %all-reduce.10 = (bf16[96]{0:T(256)(128)(2,1)S(1)}, bf16[96]{0:T(256)(128)(2,1)S(1)}, bf16[96]{0:T(256)(128)(2,1)S(1)}, bf16[96]{0:T(256)(128)(2,1)S(1)}, bf16[9...) all-reduce(bf16[96]{0:T(256)(128)(2,1)S(1)} %dynamic-slice.1, ...), channel_id=1, replica_groups=mesh['seq'=4,'batch'=8] {'seq'}, use_global_device_ids=true, to_apply=%region_19.20 | all-reduce | flops 1152 | bytes 4608 | tf_op jit(solution)/shard_map/psum | solution.py:237
  689.7 11.8 %all-reduce.14.cloned.1.call-done = (bf16[96,768]{1,0:T(8,128)(2,1)}, bf16[96,768]{1,0:T(8,128)(2,1)}, bf16[96,768]{1,0:T(8,128)(2,1)}, bf16[96,768]{1,0:T(8,128...) async-done(((bf16[96,768]{1,0:T(8,128)(2,1)}, bf16[96,768]{1,0:T(8,128)(2,1)}, bf16[96,768]{1,0:T(8,128)(2,1)}, bf16[96,768]{1,0:T(8,128)(2,1)}, ...) | async-done | bytes 1769488 | tf_op jit(solution)/shard_map/psum | solution.py:239
  (296 shorter events, 234.1 us)
Async XLA Ops:
  7.2 594.7 %reduce-scatter.13.cloned.1.call-start = ((), (), s32[]{:S(2)}) async-start(), calls=%async_computation.9 | async-start | bytes 1327104 | tf_op jit(solution)/shard_map/reduce_scatter | solution.py:211
  11.3 136.0 %copy-start.36 = (f32[768]{0:T(1024)}, f32[768]{0:T(1024)S(1)}, u32[]{:S(2)}) copy-start(f32[768]{0:T(1024)S(1)} %convert_element_type.277) | copy-start | bytes 9220
  38.0 60.4 %copy-start.29 = (bf16[672,768]{1,0:T(8,128)(2,1)S(1)}, bf16[672,768]{1,0:T(8,128)(2,1)}, u32[]{:S(2)}) copy-start(bf16[672,768]{1,0:T(8,128)(2,1)} %add_convert_fusion.4) | copy-start | bytes 3096580
  38.0 55.3 %collective-permute-start = (bf16[2,3,224,12,64]{2,4,3,1,0:T(8,128)(2,1)S(1)}, bf16[2,3,224,12,64]{2,4,3,1,0:T(8,128)(2,1)}, u32[]{:S(2)}, u32[]{:S(2)}) collective-permute-start(bf16[2,3,224,12,64]{2,4,3,1,0:T(8,128)(2,1)S(1)} %pad_maximum_fusion), channel_id=1, source_target_pairs={{0,8},{8,16},{16,24},{24,0},{1,9},{9,17},{17,25},{25,1},{2,10},{10... | collective-permute-start | bytes 6193160 | tf_op jit(solution)/shard_map/ppermute | solution.py:15
  93.3 53.6 %collective-permute-start.1 = (bf16[2,3,224,12,64]{2,4,3,1,0:T(8,128)(2,1)}, bf16[2,3,224,12,64]{2,4,3,1,0:T(8,128)(2,1)}, u32[]{:S(2)}, u32[]{:S(2)}) collective-permute-start(bf16[2,3,224,12,64]{2,4,3,1,0:T(8,128)(2,1)} %collective-permute-done), channel_id=1, source_target_pairs={{0,8},{8,16},{16,24},{24,0},{1,9},{9,17},{17,25},{25,1},{2,10},{10... | collective-permute-start | bytes 6193160 | tf_op jit(solution)/shard_map/ppermute | solution.py:15
  146.9 52.8 %collective-permute-start.2 = (bf16[2,3,224,12,64]{2,4,3,1,0:T(8,128)(2,1)}, bf16[2,3,224,12,64]{2,4,3,1,0:T(8,128)(2,1)S(1)}, u32[]{:S(2)}, u32[]{:S(2)}) collective-permute-start(bf16[2,3,224,12,64]{2,4,3,1,0:T(8,128)(2,1)} %collective-permute-done.1), channel_id=1, source_target_pairs={{0,8},{8,16},{16,24},{24,0},{1,9},{9,17},{17,25},{25,1},{2,10},{10... | collective-permute-start | bytes 6193160 | tf_op jit(solution)/shard_map/ppermute | solution.py:15
  157.2 69.3 %copy-start.5 = (f32[3,12,224,224]{3,2,1,0:T(8,128)}, f32[3,12,224,224]{3,2,1,0:T(8,128)S(1)}, u32[]{:S(2)}) copy-start(f32[3,12,224,224]{3,2,1,0:T(8,128)S(1)} %get-tuple-element.77) | copy-start | bytes 21676036
  161.4 60.5 %copy-start.4 = (f32[3,12,224,224]{3,2,1,0:T(8,128)}, f32[3,12,224,224]{3,2,1,0:T(8,128)S(1)}, u32[]{:S(2)}) copy-start(f32[3,12,224,224]{3,2,1,0:T(8,128)S(1)} %get-tuple-element.75) | copy-start | bytes 21676036
  271.3 330.7 %reduce-scatter.7.cloned.1.call-start = ((), (), s32[]{:S(2)}) async-start(), calls=%async_computation.6 | async-start | bytes 1327104 | tf_op jit(solution)/shard_map/reduce_scatter | solution.py:196
  329.7 272.3 %reduce-scatter.17.cloned.1.call-start = ((), (), s32[]{:S(2)}) async-start(), calls=%async_computation.11 | async-start | bytes 5308416 | tf_op jit(solution)/shard_map/reduce_scatter | solution.py:229
  340.5 261.5 %reduce-scatter.15.cloned.1.call-start = ((), (), s32[]{:S(2)}) async-start(), calls=%async_computation.10 | async-start | bytes 5308416 | tf_op jit(solution)/shard_map/reduce_scatter | solution.py:223
  351.9 52.0 %collective-permute-start.3 = (bf16[2,3,224,12,64]{2,4,3,1,0:T(8,128)(2,1)}, bf16[2,3,224,12,64]{2,4,3,1,0:T(8,128)(2,1)}, u32[]{:S(2)}, u32[]{:S(2)}) collective-permute-start(bf16[2,3,224,12,64]{2,4,3,1,0:T(8,128)(2,1)} %pad_maximum_fusion.1), channel_id=1, source_target_pairs={{0,8},{8,16},{16,24},{24,0},{1,9},{9,17},{17,25},{25,1},{2,10},{10... | collective-permute-start | bytes 6193160 | tf_op jit(solution)/shard_map/ppermute | solution.py:15
  358.3 243.7 %reduce-scatter.11.cloned.1.call-start = ((), (), s32[]{:S(2)}) async-start(), calls=%async_computation.8 | async-start | bytes 1327104 | tf_op jit(solution)/shard_map/reduce_scatter | solution.py:205
  362.0 46.2 %slice-start.6 = ((s8[8257536]{0:T(1024)(128)(4,1)}), s8[4194304]{0:T(1024)(128)(4,1)S(1)}, s32[]{:S(2)}) async-start(s8[8257536]{0:T(1024)(128)(4,1)} %bitcast.305), calls=%async_computation.19 | async-start | bytes 8388608
  367.7 40.5 %slice-start.7 = ((s8[8257536]{0:T(1024)(128)(4,1)}), s8[4063232]{0:T(1024)(128)(4,1)S(1)}, s32[]{:S(2)}) async-start(s8[8257536]{0:T(1024)(128)(4,1)} %bitcast.305), calls=%async_computation.20 | async-start | bytes 8126464
  406.7 50.7 %collective-permute-start.4 = (bf16[2,3,224,12,64]{2,4,3,1,0:T(8,128)(2,1)S(1)}, bf16[2,3,224,12,64]{2,4,3,1,0:T(8,128)(2,1)S(1)}, u32[]{:S(2)}, u32[]{:S(2)}) collective-permute-start(bf16[2,3,224,12,64]{2,4,3,1,0:T(8,128)(2,1)S(1)} %fusion.43), channel_id=1, source_target_pairs={{0,8},{8,16},{16,24},{24,0},{1,9},{9,17},{17,25},{25,1},{2,10},{10... | collective-permute-start | bytes 6193160 | tf_op jit(solution)/shard_map/ppermute | solution.py:15
  408.2 52.8 %slice-start.2 = ((s8[8257536]{0:T(1024)(128)(4,1)}), s8[4194304]{0:T(1024)(128)(4,1)S(1)}, s32[]{:S(2)}) async-start(s8[8257536]{0:T(1024)(128)(4,1)} %bitcast.301), calls=%async_computation.15 | async-start | bytes 8388608
  410.9 50.2 %slice-start.3 = ((s8[8257536]{0:T(1024)(128)(4,1)}), s8[4063232]{0:T(1024)(128)(4,1)S(1)}, s32[]{:S(2)}) async-start(s8[8257536]{0:T(1024)(128)(4,1)} %bitcast.301), calls=%async_computation.16 | async-start | bytes 8126464
  458.4 50.5 %collective-permute-start.5 = (bf16[2,3,224,12,64]{2,4,3,1,0:T(8,128)(2,1)S(1)}, bf16[2,3,224,12,64]{2,4,3,1,0:T(8,128)(2,1)S(1)}, u32[]{:S(2)}, u32[]{:S(2)}) collective-permute-start(bf16[2,3,224,12,64]{2,4,3,1,0:T(8,128)(2,1)S(1)} %fusion.44), channel_id=1, source_target_pairs={{0,8},{8,16},{16,24},{24,0},{1,9},{9,17},{17,25},{25,1},{2,10},{10... | collective-permute-start | bytes 6193160 | tf_op jit(solution)/shard_map/ppermute | solution.py:15
  509.8 49.0 %collective-permute-start.6 = (bf16[2,3,224,12,64]{2,4,3,1,0:T(8,128)(2,1)S(1)}, bf16[2,3,224,12,64]{2,4,3,1,0:T(8,128)(2,1)S(1)}, u32[]{:S(2)}, u32[]{:S(2)}) collective-permute-start(bf16[2,3,224,12,64]{2,4,3,1,0:T(8,128)(2,1)S(1)} %fusion.45), channel_id=1, source_target_pairs={{0,8},{8,16},{16,24},{24,0},{1,9},{9,17},{17,25},{25,1},{2,10},{10... | collective-permute-start | bytes 6193160 | tf_op jit(solution)/shard_map/ppermute | solution.py:15
  568.6 65.4 %reduce-scatter.9.cloned.1.call-start = ((), (), s32[]{:S(2)}) async-start(), calls=%async_computation.7 | async-start | bytes 1327104 | tf_op jit(solution)/shard_map/reduce_scatter | solution.py:202
  580.0 121.5 %all-reduce.14.cloned.1.call-start = ((), (), s32[]{:S(2)}) async-start(), calls=%async_computation.12 | async-start | bytes 3538944 | tf_op jit(solution)/shard_map/psum | solution.py:239
  597.7 36.4 %copy-start.41 = (f32[672]{0:T(1024)S(1)}, f32[672]{0:T(1024)}, u32[]{:S(2)}) copy-start(f32[672]{0:T(1024)} %copy-done.40) | copy-start | bytes 8068
  634.1 46.5 %copy-start.43 = (f32[672]{0:T(1024)S(1)}, f32[672]{0:T(1024)}, u32[]{:S(2)}) copy-start(f32[672]{0:T(1024)} %copy-done.42) | copy-start | bytes 8068
  (60 other events, 507.0 us)
Sparse Core Ops, SparseCore 0:
  271.4 32.5 reduce-scatter.12
  329.8 32.7 reduce-scatter.6
  364.9 53.0 reduce-scatter.16
  420.2 53.3 reduce-scatter.14
  568.8 31.7 reduce-scatter.10
  602.7 31.3 reduce-scatter.8
  637.8 63.6 all-reduce.13
where the time goes:
time: 728 us; the launch traced here: 719 us
  waiting for transfers between devices  339 us (47%)
  matrix products  183 us (25%)
  local copies, waits for them, and re-layouts  82 us (11%)
  other arithmetic  56.5 us (8%)
  blocking collectives  36.1 us (5%)
  between operations  17 us (2%)
    ppermute x7, waiting for transfers between devices, from_behind(): lax.ppermute(x, axis, [(i, (i + by) % length) for i in range(length)])  295 us
    reduce_scatter x1, waiting for transfers between devices, body(): lax.psum_scatter(grad_w_key.astype(jnp.bfloat16), 'batch', scatter_dimens...  32 us
    dot_general x6, matrix products, outer_sum(): lax.dot_general(left, right, (((0,), (0,)), ((), ())), preferred_element_...  30.2 us
    dot_general x6, matrix products, back_dot(): lax.dot_general(grad_rows, weight, (((1,), (1,)), ((), ())), preferred_el...  29.4 us
    unnamed x1, blocking collectives  26 us
    dot_general x5, matrix products, front_dot(): jnp.dot(rows_low, weight, preferred_element_type=jnp.float32)  25.4 us
    dot_general x4, matrix products, body(): jnp.einsum('srhd,sthd->srht', grad_attended, moving[1], preferred_element...  23.3 us
    dot_general x4, matrix products, body(): jnp.einsum('srht,sthd->srhd', weights_exp.astype(jnp.bfloat16), moving[1]...  20.4 us
  transfers between devices with their start and end apart: 14, of which 9 were waited for; matrix products, arithmetic and copies ran while one was open for 29% of the time, Pallas kernels for 0%

commit v1 on v0

--- a/solution.py
+++ b/solution.py
@@ -1,13 +1,553 @@
+import functools
+import math
+
 import jax
 import jax.numpy as jnp
 from jax import lax
+from jax.experimental import pallas as pl
+from jax.experimental.pallas import tpu as pltpu
 from jax.sharding import PartitionSpec as P
 
 HEAD_DIM = 64
-
-
 norm_eps = 1e-05
 masked_score = -1e30
+
+bf16 = jnp.bfloat16
+f32 = jnp.float32
+MESH = pl.DeviceIdType.MESH
+ANY = pl.BlockSpec(memory_space=pl.ANY)
+VM = pl.BlockSpec(memory_space=pltpu.VMEM)
+SM = pl.BlockSpec(memory_space=pltpu.SMEM)
+NN = (((1,), (0,)), ((), ()))
+NT = (((1,), (1,)), ((), ()))
+TN = (((0,), (0,)), ((), ()))
+LOG2E = math.log2(math.e)
+GC0 = math.sqrt(2.0 / math.pi)
+GC1 = GC0 * 0.044715
+
+
+def dg(a, b, dims):
+    return lax.dot_general(a, b, dims, preferred_element_type=f32)
+
+
+def al(i, m=16):
+    return pl.multiple_of(i, m)
+
+
+def places():
+    s = lax.axis_index("seq")
+    b = lax.axis_index("batch")
+    y, x = s // 2, s % 2
+    return s, b, y * 2 + (1 - x), (1 - y) * 2 + x, (1 - y) * 2 + (1 - x)
+
+
+def row_norm(x):
+    mean = jnp.mean(x, axis=-1, keepdims=True)
+    c = x - mean
+    r = lax.rsqrt(jnp.mean(c * c, axis=-1, keepdims=True) + norm_eps)
+    return c * r, r
+
+
+def attend_kernel(
+    C, R, D, S,
+    x_h, len_s, vec, wq_h, wk_h, wv_h,
+    n1_h, q_h, k_h, v_h, a_h, li_h, e_h,
+    x_v, n1, wq, wk, wv, q_v, k_v, v_v, a_v, li_v, e_v, s_v,
+    lsem, osem, esem, sx, sy, rx, ry, sdx, sdy, rdx, rdy,
+):
+    T = R * S
+    HR = R // 2
+    pairs = D // 128
+    s, b, px, py, pd = places()
+    bar = pltpu.get_barrier_semaphore()
+    for o in (px, py):
+        pl.semaphore_signal(bar, 1, device_id=(o, b), device_id_type=MESH)
+    xc = [
+        pltpu.make_async_copy(
+            x_h.at[pl.ds(i * R, R)], x_v.at[pl.ds(i * R, R)], lsem.at[i]
+        )
+        for i in range(C)
+    ]
+    for c in xc:
+        c.start()
+    wc = [
+        pltpu.make_async_copy(h, v, lsem.at[C + i])
+        for i, (h, v) in enumerate(((wk_h, wk), (wv_h, wv), (wq_h, wq)))
+    ]
+    for c in wc:
+        c.start()
+
+    def rows(q, blk, off, n):
+        return pl.ds(al((q * S + blk) * R + off), n)
+
+    def own_copy(q, peer, ss, rs):
+        ref = n1.at[rows(q, s, 0, R)]
+        return pltpu.make_async_remote_copy(
+            ref, ref, ss.at[q], rs.at[q], device_id=(peer, b), device_id_type=MESH
+        )
+
+    def relay_copy(q, peer, blk, off, ss, rs):
+        ref = n1.at[rows(q, blk, off, HR)]
+        return pltpu.make_async_remote_copy(
+            ref, ref, ss.at[q], rs.at[q], device_id=(peer, b), device_id_type=MESH
+        )
+
+    own = [(own_copy(q, px, sx, rx), own_copy(q, py, sy, ry)) for q in range(C)]
+    rel = [
+        (relay_copy(q, py, px, 0, sdy, rdy), relay_copy(q, px, py, HR, sdx, rdx))
+        for q in range(C)
+    ]
+
+    gain, shift = vec[0:1, :], vec[1:2, :]
+    bq, bv = vec[2:3, :], vec[3:4, :]
+    for q in range(C):
+        xc[q].wait()
+        z, _ = row_norm(x_v[q * R : (q + 1) * R, :].astype(f32))
+        n1[rows(q, s, 0, R), :] = (z * gain + shift).astype(bf16)
+        if q == 0:
+            pl.semaphore_wait(bar, 2)
+        if q < 2:
+            for c in own[q]:
+                c.start()
+    for c in wc:
+        c.wait()
+
+    def kv(q, blk):
+        rs = rows(q, blk, 0, R)
+        v = n1[rs, :]
+        k_v[rs, :] = dg(v, wk[...], NN).astype(bf16)
+        v_v[rs, :] = (dg(v, wv[...], NN) + bv).astype(bf16)
+
+    def own_rows(q, _):
+        v = n1[rows(q, s, 0, R), :]
+        q_v[pl.ds(al(q * R), R), :] = (
+            (dg(v, wq[...], NN) + bq) * (HEAD_DIM ** (-0.5) * LOG2E)
+        ).astype(bf16)
+        kv(q, s)
+        return 0
+
+    lax.fori_loop(0, C, own_rows, 0)
+    qc = pltpu.make_async_copy(q_v, q_h, osem.at[0])
+    qc.start()
+
+    def arrived(q):
+        for c in own[q]:
+            c.wait_recv()
+        for c in rel[q]:
+            c.start()
+
+    def near(q):
+        lax.fori_loop(0, 2, lambda i, c: (kv(q, jnp.where(i == 0, px, py)), c)[1], 0)
+
+    def far(q):
+        for c in rel[q]:
+            c.wait_recv()
+        kv(q, pd)
+        for i, (v, h) in enumerate(((n1, n1_h), (k_v, k_h), (v_v, v_h))):
+            pltpu.make_async_copy(
+                v.at[pl.ds(q * T, T)], h.at[pl.ds(q * T, T)], osem.at[3 + 3 * q + i]
+            ).start()
+
+    arrived(0)
+    for c in own[2]:
+        c.start()
+    near(0)
+    arrived(1)
+    near(1)
+    far(0)
+
+    lane = lax.broadcasted_iota(jnp.int32, (1, 128), 1)
+    lo = lane < 64
+    col = lax.broadcasted_iota(jnp.int32, (1, T), 1)
+
+    def e_copy(t):
+        return pltpu.make_async_copy(e_v.at[t % 2], e_h.at[t], esem.at[t % 2])
+
+    def pair(t, _):
+        q, p = t // pairs, t % pairs
+
+        @pl.when(t == pairs // 2)
+        def _():
+            arrived(2)
+            near(2)
+
+        for i in range(1, C):
+
+            @pl.when(t == i * pairs)
+            def _():
+                far(i)
+
+        off = al(p * 128, 128)
+        rq = pl.ds(al(q * R), R)
+        rk = pl.ds(al(q * T), T)
+        qp = q_v[rq, pl.ds(off, 128)]
+        zero = jnp.zeros_like(qp)
+        qs = jnp.concatenate([jnp.where(lo, qp, zero), jnp.where(lo, zero, qp)], 0)
+        bias = jnp.where(col < len_s[q], 0.0, masked_score).astype(f32)
+        s_v[...] = dg(qs, k_v[rk, pl.ds(off, 128)], NT) + bias
+        m = jnp.max(s_v[...], axis=1, keepdims=True)
+        e = jnp.exp2(s_v[...] - m)
+        eb = e.astype(bf16)
+        tot = jnp.sum(e, axis=1, keepdims=True)
+
+        @pl.when(t >= 2)
+        def _():
+            e_copy(t - 2).wait()
+
+        e_v[t % 2] = eb
+        e_copy(t).start()
+        ol = dg(eb, v_v[rk, pl.ds(off, 128)], NN)
+        inv = 1.0 / tot
+        inv = jnp.where(lo, inv[:R], inv[R:])
+        li_v[rq, pl.ds(off, 128)] = inv
+        a_v[rq, pl.ds(off, 128)] = (jnp.where(lo, ol[:R], ol[R:]) * inv).astype(bf16)
+        return 0
+
+    lax.fori_loop(0, C * pairs, pair, 0)
+    ac = pltpu.make_async_copy(a_v, a_h, osem.at[1])
+    lc = pltpu.make_async_copy(li_v, li_h, osem.at[2])
+    ac.start()
+    lc.start()
+    e_copy(C * pairs - 2).wait()
+    e_copy(C * pairs - 1).wait()
+    for q in range(C):
+        for i, (v, h) in enumerate(((n1, n1_h), (k_v, k_h), (v_v, v_h))):
+            pltpu.make_async_copy(
+                v.at[pl.ds(q * T, T)], h.at[pl.ds(q * T, T)], osem.at[3 + 3 * q + i]
+            ).wait()
+        for c in own[q] + rel[q]:
+            c.wait_send()
+    qc.wait()
+    ac.wait()
+    lc.wait()
+
+
+def attend(C, R, D, S, x, lengths, vec, wq, wk, wv):
+    N, T, pairs = C * R, R * S, D // 128
+    sd = jax.ShapeDtypeStruct
+    dma = pltpu.SemaphoreType.DMA
+    return pl.pallas_call(
+        functools.partial(attend_kernel, C, R, D, S),
+        out_shape=(
+            sd((C * T, D), bf16),
+            sd((N, D), bf16),
+            sd((C * T, D), bf16),
+            sd((C * T, D), bf16),
+            sd((N, D), bf16),
+            sd((N, D), f32),
+            sd((C * pairs, 2 * R, T), bf16),
+        ),
+        in_specs=[ANY, SM, VM, ANY, ANY, ANY],
+        out_specs=(ANY,) * 7,
+        scratch_shapes=[
+            pltpu.VMEM((N, D), bf16),
+            pltpu.VMEM((C * T, D), bf16),
+            pltpu.VMEM((D, D), bf16),
+            pltpu.VMEM((D, D), bf16),
+            pltpu.VMEM((D, D), bf16),
+            pltpu.VMEM((N, D), bf16),
+            pltpu.VMEM((C * T, D), bf16),
+            pltpu.VMEM((C * T, D), bf16),
+            pltpu.VMEM((N, D), bf16),
+            pltpu.VMEM((N, D), f32),
+            pltpu.VMEM((2, 2 * R, T), bf16),
+            pltpu.VMEM((2 * R, T), f32),
+            dma((C + 3,)),
+            dma((3 + 3 * C,)),
+            dma((2,)),
+        ]
+        + [dma((C,))] * 8,
+        compiler_params=pltpu.CompilerParams(
+            collective_id=1, has_side_effects=True, vmem_limit_bytes=60 * 2**20
+        ),
+        cost_estimate=pl.CostEstimate(
+            flops=20 * 10**9, bytes_accessed=40 * 10**6, transcendentals=0
+        ),
+    )(x, lengths, vec, wq, wk, wv)
+
+
+def backward_kernel(
+    C, R, D, S, FF,
+    x_h, cot_h, a_h, li_h, q_h, k_h, v_h, n1_h, e_h, vec, bup, wo_h, wu_h, wd_h, wq_h, wk_h, wv_h,
+    out_h, dh_h, g_h, dn_h, sm_h,
+    x_v, cot, a_v, q_v, n2, pb, du, h_v, acc, dn2, kk, vv, n1, wq, wk, wv, wo, gb, dn, e_v, sm, lsem, esem, osem,
+):
+    T, N = R * S, C * R
+    pairs = D // 128
+    J = FF // D
+    B = 8
+    CH = D // B
+    s, b, px, py, pd = places()
+    t_rows = C * T
+
+    def load(i, h, v):
+        c = pltpu.make_async_copy(h, v, lsem.at[i])
+        c.start()
+        return c
+
+    c_a = load(0, a_h, a_v)
+    c_wo = load(1, wo_h, wo)
+    c_x = load(2, x_h, x_v)
+    c_cot = load(3, cot_h, cot)
+    c_w = [
+        (
+            load(4 + 2 * j, wu_h.at[:, pl.ds(j * D, D)], vv.at[pl.ds(j * D, D)]),
+            load(5 + 2 * j, wd_h.at[pl.ds(j * D, D)], kk.at[pl.ds(j * D, D)]),
+        )
+        for j in range(J)
+    ]
+    n0 = 4 + 2 * J
+    c_q = load(n0, q_h, q_v)
+    c_n1 = load(n0 + 1, n1_h, n1)
+    c_wk = load(n0 + 2, wk_h, wk)
+    c_wv = load(n0 + 3, wv_h, wv)
+    c_wq = load(n0 + 4, wq_h, wq)
+
+    def e_copy(t, slot):
+        return pltpu.make_async_copy(e_h.at[t], e_v.at[slot], esem.at[slot])
+
+    e_copy(0, 0).start()
+    e_copy(1, 1).start()
+
+    gain1, shift1 = vec[0:1, :], vec[1:2, :]
+    b_out, gain2, shift2, b_down = vec[4:5, :], vec[5:6, :], vec[6:7, :], vec[7:8, :]
+    sm[...] = jnp.zeros_like(sm)
+    for c in (c_a, c_wo, c_x, c_cot):
+        c.wait()
+
+    def first(i, _):
+        r = pl.ds(al(i * R), R)
+        h = x_v[r, :].astype(f32) + dg(a_v[r, :], wo[...], NN) + b_out
+        h_v[r, :] = h
+        z, _r = row_norm(h)
+        n2[r, :] = (z * gain2 + shift2).astype(bf16)
+        acc[r, :] = h + b_down
+        dn2[r, :] = jnp.zeros((R, D), f32)
+        sm[7:8, :] += jnp.sum(cot[r, :].astype(f32), axis=0, keepdims=True)
+        return 0
+
+    lax.fori_loop(0, C, first, 0)
+
+    def ffn(j, _):
+        jr = pl.ds(al(j * D), D)
+        for jj in range(J):
+
+            @pl.when(j == jj)
+            def _():
+                c_w[jj][0].wait()
+                c_w[jj][1].wait()
+
+        bias = bup[pl.ds(j, 1), :]
+
+        def chunk(i, sums):
+            r = pl.ds(al(i * R), R)
+            u = dg(n2[r, :], vv[jr, :], NN) + bias
+            g = dg(cot[r, :], kk[jr, :], NT)
+            u2 = u * u
+            t = jnp.tanh(u * (GC0 + GC1 * u2))
+            hu = 0.5 * u
+            half = 0.5 + 0.5 * t
+            p = (u * half).astype(bf16)
+            d = (g * (half + hu * (1.0 - t * t) * (GC0 + 3.0 * GC1 * u2))).astype(bf16)
+            pb[r, :] = p
+            du[r, :] = d
+            acc[r, :] += dg(p, kk[jr, :], NN)
+            dn2[r, :] += dg(d, vv[jr, :], NT)
+            return sums + jnp.sum(d.astype(f32), axis=0, keepdims=True)
+
+        sm[pl.ds(8 + j, 1), :] = lax.fori_loop(0, C, chunk, jnp.zeros((1, D), f32))
+        gb[j] = dg(n2[...], du[...], TN).astype(bf16).reshape(B // 2, 2, CH, D)
+        gw = dg(pb[...], cot[...], TN).astype(bf16)
+        per = FF // B
+        for bb in range(D // per):
+            for i in range(per // CH):
+                o = bb * per + i * CH
+                gb[J + i, j, bb] = gw[o : o + CH, :]
+        return 0
+
+    lax.fori_loop(0, J, ffn, 0)
+
+    c_k = load(0, k_h, kk.at[pl.ds(0, t_rows)])
+    c_v = load(1, v_h, vv.at[pl.ds(0, t_rows)])
+
+    def second(i, _):
+        r = pl.ds(al(i * R), R)
+        pb[r, :] = acc[r, :].astype(bf16)
+        z, rr = row_norm(h_v[r, :])
+        dn = dn2[r, :]
+        g = dn * gain2
+        sm[5:6, :] += jnp.sum(dn * z, axis=0, keepdims=True)
+        sm[6:7, :] += jnp.sum(dn, axis=0, keepdims=True)
+        dh = cot[r, :].astype(f32) + rr * (
+            g
+            - jnp.mean(g, axis=-1, keepdims=True)
+            - z * jnp.mean(g * z, axis=-1, keepdims=True)
+        )
+        h_v[r, :] = dh
+        db = dh.astype(bf16)
+        n2[r, :] = db
+        sm[4:5, :] += jnp.sum(db.astype(f32), axis=0, keepdims=True)
+        du[r, :] = dg(db, wo[...], NT).astype(bf16)
+        return 0
+
+    lax.fori_loop(0, C, second, 0)
+    c_li = load(2, li_h, acc)
+    c_o = pltpu.make_async_copy(pb, out_h, osem.at[0])
+    c_o.start()
+    c_dh = pltpu.make_async_copy(h_v, dh_h, osem.at[1])
+    c_dh.start()
+    gb[2 * J] = dg(a_v[...], n2[...], TN).astype(bf16).reshape(B // 2, 2, CH, D)
+
+    for c in (c_k, c_v, c_li, c_q, c_wk, c_wv, c_wq, c_n1):
+        c.wait()
+    dq_v, do_v = cot, du
+    lane = lax.broadcasted_iota(jnp.int32, (1, 128), 1)
+    lo = lane < 64
+
+    def stack(v):
+        zero = jnp.zeros_like(v)
+        return jnp.concatenate([jnp.where(lo, v, zero), jnp.where(lo, zero, v)], 0)
+
+    def pair(t, _):
+        q, p = t // pairs, t % pairs
+        slot = t % 2
+        lanes = pl.ds(al(p * 128, 128), 128)
+        rq = pl.ds(al(q * R), R)
+        rk = pl.ds(al(q * T), T)
+        qs = stack(q_v[rq, lanes])
+        dof = do_v[rq, lanes].astype(f32) * acc[rq, lanes]
+        dos = stack(dof.astype(bf16))
+        dl = jnp.sum(stack(dof * a_v[rq, lanes].astype(f32)), axis=1, keepdims=True)
+        e_copy(t, slot).wait()
+        dp = dg(dos, vv[rk, lanes], NT)
+        ds = (e_v[slot].astype(f32) * (dp - dl)).astype(bf16)
+        dqs = dg(ds, kk[rk, lanes], NN)
+        dq_v[rq, lanes] = (jnp.where(lo, dqs[:R], dqs[R:]) * (HEAD_DIM ** (-0.5))).astype(
+            bf16
+        )
+        kk[rk, lanes] = (dg(qs, ds, TN) * (1.0 / LOG2E)).astype(bf16).T
+        vv[rk, lanes] = dg(dos, e_v[slot], TN).astype(bf16).T
+
+        @pl.when(t + 2 < C * pairs)
+        def _():
+            e_copy(t + 2, slot).start()
+
+        @pl.when(p == pairs - 1)
+        def _():
+            def block(i, _):
+                blk = (s + 1 + i) % S
+                rr = pl.ds(al((q * S + blk) * R), R)
+                f = dg(kk[rr, :], wk[...], NT) + dg(vv[rr, :], wv[...], NT)
+                f += jnp.where(blk == s, 1.0, 0.0) * dg(dq_v[rq, :], wq[...], NT)
+                n = n1[rr, :].astype(f32)
+                sm[0:1, :] += jnp.sum(f * n, axis=0, keepdims=True)
+                sm[1:2, :] += jnp.sum(f, axis=0, keepdims=True)
+                dn[rr, :] = f.astype(bf16)
+                return 0
+
+            lax.fori_loop(0, S, block, 0)
+
+        return 0
+
+    lax.fori_loop(0, C * pairs, pair, 0)
+    c_dn = pltpu.make_async_copy(dn, dn_h, osem.at[2])
+    c_dn.start()
+    sm[0:1, :] = (sm[0:1, :] - shift1 * sm[1:2, :]) / gain1
+    sm[2:3, :] = jnp.sum(dq_v[...].astype(f32), axis=0, keepdims=True)
+    sm[3:4, :] = jnp.sum(vv[0:t_rows, :].astype(f32), axis=0, keepdims=True)
+    for i in range(C):
+        r = pl.ds(i * R, R)
+        x_v[r, :] = n1[pl.ds(al((i * S + s) * R), R), :]
+    gb[2 * J + 1] = dg(x_v[...], dq_v[...], TN).astype(bf16).reshape(B // 2, 2, CH, D)
+    gb[2 * J + 2] = dg(n1[...], kk[0:t_rows, :], TN).astype(bf16).reshape(B // 2, 2, CH, D)
+    gb[2 * J + 3] = dg(n1[...], vv[0:t_rows, :], TN).astype(bf16).reshape(B // 2, 2, CH, D)
+    c_g = pltpu.make_async_copy(gb, g_h, osem.at[3])
+    c_g.start()
+    c_s = pltpu.make_async_copy(sm, sm_h, osem.at[4])
+    c_s.start()
+    for c in (c_o, c_dh, c_dn, c_g, c_s):
+        c.wait()
+
+
+def backward(C, R, D, S, FF, x, cot, a, li, q, k, v, n1, e, vec, bup, wo, wu, wd, wq, wk, wv):
+    N, T = C * R, R * S
+    J = FF // D
+    U = 2 * J + 4
+    sd = jax.ShapeDtypeStruct
+    dma = pltpu.SemaphoreType.DMA
+    vm = pltpu.VMEM
+    return pl.pallas_call(
+        functools.partial(backward_kernel, C, R, D, S, FF),
+        out_shape=(
+            sd((N, D), bf16),
+            sd((N, D), f32),
+            sd((U, 4, 2, D // 8, D), bf16),
+            sd((C * T, D), bf16),
+            sd((16, D), f32),
+        ),
+        in_specs=[ANY] * 9 + [VM, VM] + [ANY] * 6,
+        out_specs=(ANY,) * 5,
+        scratch_shapes=[
+            vm((N, D), bf16), vm((N, D), bf16), vm((N, D), bf16), vm((N, D), bf16),
+            vm((N, D), bf16), vm((N, D), bf16), vm((N, D), bf16),
+            vm((N, D), f32), vm((N, D), f32), vm((N, D), f32),
+            vm((FF, D), bf16), vm((FF, D), bf16), vm((C * T, D), bf16),
+            vm((D, D), bf16), vm((D, D), bf16), vm((D, D), bf16), vm((D, D), bf16),
+            vm((U, 4, 2, D // 8, D), bf16), vm((C * T, D), bf16),
+            vm((2, 2 * R, T), bf16), vm((16, D), f32),
+            dma((4 + 2 * J + 5,)), dma((2,)), dma((5,)),
+        ],
+        compiler_params=pltpu.CompilerParams(vmem_limit_bytes=62 * 2**20),
+        cost_estimate=pl.CostEstimate(
+            flops=40 * 10**9, bytes_accessed=60 * 10**6, transcendentals=0
+        ),
+    )(x, cot, a, li, q, k, v, n1, e, vec, bup, wo, wu, wd, wq, wk, wv)
+
+
+def fast_body(
+    inputs, lengths, gain_one, shift_one, w_query, b_query, w_key, w_value, b_value, w_out, b_out,
+    gain_two, shift_two, w_up, b_up, w_down, b_down, cotangent,
+):
+    C, R, D = inputs.shape
+    S = lax.axis_size("seq")
+    FF = w_up.shape[1]
+    N = C * R
+    x = inputs.reshape(N, D)
+    cot = cotangent.reshape(N, D)
+    vec = jnp.stack(
+        (gain_one, shift_one, b_query, b_value, b_out, gain_two, shift_two, b_down)
+    ).astype(f32)
+    bup = b_up.reshape(FF // D, D).astype(f32)
+    n1, q, k, v, a, li, e = attend(C, R, D, S, x, lengths, vec, w_query, w_key, w_value)
+    out, dh, g, dn, sm = backward(
+        C, R, D, S, FF, x, cot, a, li, q, k, v, n1, e, vec, bup, w_out, w_up, w_down,
+        w_query, w_key, w_value,
+    )
+    dn = lax.psum_scatter(
+        dn.reshape(C, S, R, D), "seq", scatter_dimension=1, tiled=True
+    ).reshape(N, D).astype(f32)
+    z, r = row_norm(x.astype(f32))
+    gg = dn * gain_one.astype(f32)
+    dx = r * (
+        gg - jnp.mean(gg, axis=-1, keepdims=True) - z * jnp.mean(gg * z, axis=-1, keepdims=True)
+    )
+    input_grad = (dh + dx).astype(bf16)
+    sm = lax.psum(sm, ("seq", "batch"))
+    b = lax.axis_index("batch")
+    U = g.shape[0]
+    g = lax.psum_scatter(g.reshape(U, 8, D // 8, D), "batch", scatter_dimension=1, tiled=True)
+    g = lax.psum(g, "seq").reshape(U, D // 8, D).astype(f32)
+    J = FF // D
+    part = D // 8
+    small = lax.dynamic_slice(sm, (0, b * part), (8, part))
+    up = jnp.concatenate([g[i] for i in range(J)], axis=1)
+    down = g[J : 2 * J].reshape(FF // 8, D)
+    gbup = lax.dynamic_slice(sm[8 : 8 + J].reshape(FF), (b * (FF // 8),), (FF // 8,))
+    return (
+        out.reshape(inputs.shape), input_grad.reshape(inputs.shape),
+        small[0], small[1], g[2 * J + 1], small[2], g[2 * J + 2], g[2 * J + 3], small[3],
+        g[2 * J], small[4], small[5], small[6], up, gbup, down, small[7],
+    )
 
 
 def from_behind(x, axis, by):
@@ -54,7 +594,7 @@
     return jnp.where(valid, scores, masked_score)
 
 
-def body(
+def ring_body(
     inputs,
     lengths,
     gain_one,
@@ -292,6 +832,8 @@
         P(),
         P("batch", "seq", None),
     )
+    small = mesh.shape["seq"] == 4 and mesh.shape["batch"] == 8
+    body = fast_body if small else ring_body
     return jax.shard_map(
         body,
         mesh=mesh,

time: 728 us -> 524 us (0.72); the launches traced: 719 us -> 523 us
  matrix products: 183 us -> 0 us
  Pallas kernels: 0 us -> 141 us
  local copies, waits for them, and re-layouts: 82 us -> 20.7 us
  other arithmetic: 56.5 us -> 9.57 us
  waiting for transfers between devices: 339 us -> 295 us
    ppermute x7 -> x0, waiting for transfers between devices: 295 us -> none  [from_behind(): lax.ppermute(x, axis, [(i, (i + by) % length) for i in range(length)])]
    unnamed x7 -> x5, waiting for transfers between devices: 0.11 us -> 279 us
    dot_general x42 -> x0, matrix products: 183 us -> none  [the longest x6 30.2 us: outer_sum(): lax.dot_general(left, right, (((0,), (0,)), ((), ())), preferred_element_...]
    pallas_call x0 -> x2, Pallas kernels: none -> 141 us  [the longest x1 83.3 us: backward(): pl.pallas_call(functools.partial(backward_kernel, C, R, D, S, FF), out_sh...]
    reduce_scatter x6 -> x0, waiting for transfers between devices: 32.1 us -> none  [the longest x1 32 us: body(): lax.psum_scatter(grad_w_key.astype(jnp.bfloat16), 'batch', scatter_dimens...]
    psum x1, blocking collectives: 10.1 us -> 40.7 us  [fast_body(): sm = lax.psum(sm, ('seq', 'batch'))]
    unnamed x1 -> x0, blocking collectives: 26 us -> none
    convert_element_type x8 -> x1, local copies, waits for them, and re-layouts: 24.8 us -> 1.3 us  [fast_body(): bup = b_up.reshape(FF // D, D).astype(f32)]
  transfers between devices with their start and end apart: 14 -> 3, of which waited for: 9 -> 2; matrix products, arithmetic and copies ran while one was open for 29% -> 3% of each run, Pallas kernels for 0% -> 0%
where the time goes in v1:
time: 524 us; the launch traced here: 523 us
  waiting for transfers between devices  295 us (56%)
  Pallas kernels  141 us (27%)
  blocking collectives  40.7 us (8%)
  local copies, waits for them, and re-layouts  20.7 us (4%)
  between operations  15.6 us (3%)
  other arithmetic  9.57 us (2%)
    unnamed x5, waiting for transfers between devices  279 us
    pallas_call x1, Pallas kernels, backward(): pl.pallas_call(functools.partial(backward_kernel, C, R, D, S, FF), out_sh...  83.3 us
    pallas_call x1, Pallas kernels, attend(): pl.pallas_call(functools.partial(attend_kernel, C, R, D, S), out_shape=(s...  57.9 us
    psum x1, blocking collectives, fast_body(): sm = lax.psum(sm, ('seq', 'batch'))  40.7 us
    psum x1, waiting for transfers between devices, fast_body(): g = lax.psum(g, 'seq').reshape(U, D // 8, D).astype(f32)  16.4 us
  transfers between devices with their start and end apart: 3, of which 2 were waited for; matrix products, arithmetic and copies ran while one was open for 3% of the time, Pallas kernels for 0%

profile of v1, /device:TPU:0, one launch (start us, length us, event | category | flops | bytes accessed | tf_op | source)
XLA Modules:
  0.0 523.0 jit_solution(6452568939235448445)
XLA Ops:
  8.1 0.7 stack.27
  8.8 0.7 stack.28
  9.4 0.7 stack.29
  10.1 0.7 stack.30
  10.8 0.7 stack.31
  11.5 0.7 stack.32
  12.2 0.7 stack.33
  12.9 0.7 stack.34
  14.2 1.3 reshape.175.bup
  15.5 57.9 %shard_map.305 = (bf16[2688,768]{1,0:T(8,128)(2,1)}, bf16[672,768]{1,0:T(8,128)(2,1)}, bf16[2688,768]{1,0:T(8,128)(2,1)}, bf16[2688,768]{1,0:T(8,128)(2,1)}, bf1...) custom-call(bf16[672,768]{1,0:T(8,128)(2,1)} %bitcast.66, s32[3]{0:T(128)} %len_s.1, ...), custom_call_target="tpu_custom_call" | custom-call | flops 20000000000 | bytes 40000000 | tf_op jit(solution)/shard_map/pallas_call | solution.py:229
  73.4 83.3 %shard_map.306 = (bf16[672,768]{1,0:T(8,128)(2,1)}, f32[672,768]{1,0:T(8,128)}, bf16[12,4,2,96,768]{4,3,2,1,0:T(8,128)(2,1)}, bf16[2688,768]{1,0:T(8,128)(2,1)}, f32[16,768]{1,0:T(8,128)}) custom-call(bf16[672,768]{1,0:T(8,128)(2,1)} %bitcast.67, bf16[672,768]{1,0:T(8,128)(2,1)} %bitcast.72, bf16[672,768]{1,0:T(8,128)(2,1)} %get-tuple-element.29.a_h, ...), custom_call_target="tpu_custom_call" | custom-call | flops 40000000000 | bytes 60000000 | tf_op jit(solution)/shard_map/pallas_call | solution.py:479
  156.8 4.4 copy.36
  162.7 278.7 %all-reduce.7.cloned.1.call-done = bf16[12,8,96,768]{3,2,1,0:T(8,128)(2,1)} async-done(((bf16[12,8,96,768]{3,2,1,0:T(8,128)(2,1)}), bf16[12,8,96,768]{3,2,1,0:T(8,128)(2,1)}) %all-reduce.7.cloned.1.call-update) | async-done | bytes 14155792
  441.4 3.5 constant_dynamic-slice_fusion
  445.7 40.7 %psum.14 = f32[16,768]{1,0:T(8,128)S(1)} all-reduce(f32[16,768]{1,0:T(8,128)S(1)} %copy-done.3), channel_id=1, replica_groups=mesh['seq'=4,'batch'=8] {'seq','batch'}, use_global_device_ids=true, to_apply=%region_5.0 | all-reduce | flops 12288 | bytes 98304 | tf_op jit(solution)/shard_map/psum | solution.py:535
  486.5 0.7 dynamic_slice.7
  487.8 2.1 multiply_reduce_fusion
  490.0 3.3 fusion.10
  493.3 16.4 %all-reduce.5.cloned.1.call-done = bf16[12,1,96,768]{3,2,1,0:T(8,128)(2,1)} async-done(((bf16[12,1,96,768]{3,2,1,0:T(8,128)(2,1)}), bf16[12,1,96,768]{3,2,1,0:T(8,128)(2,1)}) %all-reduce.5.cloned.1.call-update) | async-done | bytes 1769488 | tf_op jit(solution)/shard_map/psum | solution.py:539
  509.7 1.8 convert_element_type.47
  511.5 1.1 slice_bitcast_fusion.3
  512.6 1.1 pad_maximum_fusion
  513.7 0.8 copy-done.1
  514.5 1.1 slice.90
  (35 shorter events, 3.8 us)
Async XLA Ops:
  8.0 433.4 %all-reduce.7.cloned.1.call-start = ((), (), s32[]{:S(2)}) async-start(), calls=%async_computation.2 | async-start | bytes 28311552
  156.8 331.0 %reduce-scatter.7.cloned.1.call-start = ((), (), s32[]{:S(2)}) async-start(), calls=%async_computation.3 | async-start | bytes 5160960
  161.2 0.7 copy-start.4
  161.2 0.7 copy-start.5
  161.2 1.3 copy-start
  161.2 348.5 %all-reduce.5.cloned.1.call-start = ((), (), s32[]{:S(2)}) async-start(), calls=%async_computation.1 | async-start | bytes 3538944 | tf_op jit(solution)/shard_map/psum | solution.py:539
  444.9 0.8 copy-start.3
  487.8 2.2 copy-start.2
  512.6 1.9 copy-start.1
Sparse Core Ops, SparseCore 0:
  156.9 284.4 all-reduce.6
Sparse Core Ops, SparseCore 1:
  161.3 52.3 reduce-scatter.6
  445.1 64.6 all-reduce.4

commit v2 on v1

--- a/solution.py
+++ b/solution.py
@@ -269,8 +269,10 @@
 def backward_kernel(
     C, R, D, S, FF,
     x_h, cot_h, a_h, li_h, q_h, k_h, v_h, n1_h, e_h, vec, bup, wo_h, wu_h, wd_h, wq_h, wk_h, wv_h,
-    out_h, dh_h, g_h, dn_h, sm_h,
-    x_v, cot, a_v, q_v, n2, pb, du, h_v, acc, dn2, kk, vv, n1, wq, wk, wv, wo, gb, dn, e_v, sm, lsem, esem, osem,
+    out_h, ig_h, f_h, sm_h,
+    cot, a_v, q_v, n2, pb, du, h_v, acc, dn2, kk, vv, n1, wk, wv, wo, gb, dn, e_v, sm,
+    rc, r2, r3, s3, r4, f, d1, d2, mc, mz, mx,
+    lsem, esem, osem, sems, rems, zs, zr, ds_s, ds_r, ms, mr, cr,
 ):
     T, N = R * S, C * R
     pairs = D // 128
@@ -278,16 +280,160 @@
     B = 8
     CH = D // B
     s, b, px, py, pd = places()
+    y, x = s // 2, s % 2
+    z, c = b // 2, b % 2
+    sib = z * 2 + 1 - c
     t_rows = C * T
+    HC, HR = CH // 2, R // 2
+    U = 2 * J + 4
+    bar = pltpu.get_barrier_semaphore()
+    beside = [(px, b), (py, b), (s, sib)] + [(s, (z + k) % 4 * 2 + c) for k in (1, 2, 3)]
+    for o in beside:
+        pl.semaphore_signal(bar, 1, device_id=o, device_id_type=MESH)
+
+    def remote(src, dst, ss, rs, dev):
+        return pltpu.make_async_remote_copy(
+            src, dst, ss, rs, device_id=dev, device_id_type=MESH
+        )
+
+    def slot(u):
+        return u - 2 * J * (u // (2 * J))
+
+    def mine(u):
+        return x + (u % 2) * (y - x)
+
+    def first_peer(u):
+        return px + (u % 2) * (py - px)
+
+    def last_peer(u):
+        return py + (u % 2) * (px - py)
+
+    def half(h):
+        return pl.ds(al(h * HC), HC)
+
+    def cp1(u):
+        return remote(gb.at[slot(u), :, 1 - c], rc.at[u % 4], sems.at[0, u], rems.at[0, u], (s, sib))
+
+    def cp2(u):
+        return remote(
+            gb.at[slot(u), :, c, half(1 - mine(u))], r2.at[slot(u)], sems.at[1, u], rems.at[1, u],
+            (first_peer(u), b),
+        )
+
+    def cp3(u, k):
+        zz = (z + k) % 4
+        return remote(
+            gb.at[slot(u), zz, c, half(mine(u))], r3.at[u, k - 1], zs.at[k - 1, u], zr.at[k - 1, u],
+            (s, zz * 2 + c),
+        )
+
+    def cp4(u):
+        return remote(s3.at[u % 4], r4.at[u], sems.at[2, u], rems.at[2, u], (last_peer(u), b))
+
+    def cp5(u):
+        ref = f.at[u, half(mine(u))]
+        return remote(ref, ref, sems.at[3, u], rems.at[3, u], (first_peer(u), b))
+
+    def sent(u):
+        cp1(u).wait_send()
+        cp2(u).wait_send()
+        for k in (1, 2, 3):
+            cp3(u, k).wait_send()
+
+    def step1(u, again):
+        if again:
+            pl.semaphore_wait(cr.at[u % 4], 1)
+        cp1(u).start()
+
+    def step2(u, more):
+        cp1(u).wait_recv()
+        gb[slot(u), :, c] += rc[u % 4]
+        if more:
+            pl.semaphore_signal(cr.at[u % 4], 1, device_id=(s, sib), device_id_type=MESH)
+        cp2(u).start()
+
+    def step3(u):
+        cp2(u).wait_recv()
+        gb[slot(u), :, c, half(mine(u))] += r2[slot(u)]
+        for k in (1, 2, 3):
+            cp3(u, k).start()
+
+    def step4(u):
+        for k in (1, 2, 3):
+            cp3(u, k).wait_recv()
+        if isinstance(u, int):
+            if u >= 4:
+                cp4(u - 4).wait_send()
+        else:
+
+            @pl.when(u >= 4)
+            def _():
+                cp4(u - 4).wait_send()
+
+        v = gb[slot(u), z, c, half(mine(u))].astype(f32)
+        for k in range(3):
+            v += r3[u, k].astype(f32)
+        s3[u % 4] = v.astype(bf16)
+        cp4(u).start()
+
+    def step5(u):
+        cp4(u).wait_recv()
+        f[u, half(mine(u))] = s3[u % 4] + r4[u]
+        cp5(u).start()
+
+    def dcp(q, i):
+        sl = q % 2
+        if i == 0:
+            a, o, dev = dn.at[sl, :, 1 - x, pl.ds(0, HR)], d1.at[sl, 0], px
+        elif i == 1:
+            a, o, dev = dn.at[sl, 1 - y, :, pl.ds(HR, HR)], d1.at[sl, 1], py
+        elif i == 2:
+            a, o, dev = dn.at[sl, 1 - y, x, pl.ds(0, HR)], d2.at[q, 0], py
+        else:
+            a, o, dev = dn.at[sl, y, 1 - x, pl.ds(HR, HR)], d2.at[q, 1], px
+        return remote(a, o, ds_s.at[i, q], ds_r.at[i, q], (dev, b))
+
+    def rows1(q):
+        dcp(q, 0).start()
+        dcp(q, 1).start()
+
+    def rows2(q):
+        sl = q % 2
+        dcp(q, 0).wait_recv()
+        dcp(q, 1).wait_recv()
+        dn[sl, :, x, 0:HR] += d1[sl, 0]
+        dn[sl, y, :, HR:R] += d1[sl, 1]
+        dcp(q, 2).start()
+        dcp(q, 3).start()
+
+    def rows3(q):
+        sl = q % 2
+        dcp(q, 2).wait_recv()
+        dcp(q, 3).wait_recv()
+        for i in range(2):
+            d = dn[sl, y, x, i * HR : (i + 1) * HR].astype(f32) + d2[q, i].astype(f32)
+            r = pl.ds(al(q * R + i * HR), HR)
+            zz, rr = row_norm(n2[r, :].astype(f32))
+            g = d * gain1
+            pb[r, :] = (
+                h_v[r, :]
+                + rr
+                * (
+                    g
+                    - jnp.mean(g, axis=-1, keepdims=True)
+                    - zz * jnp.mean(g * zz, axis=-1, keepdims=True)
+                )
+            ).astype(bf16)
+
 
     def load(i, h, v):
-        c = pltpu.make_async_copy(h, v, lsem.at[i])
-        c.start()
-        return c
+        cp = pltpu.make_async_copy(h, v, lsem.at[i])
+        cp.start()
+        return cp
 
     c_a = load(0, a_h, a_v)
     c_wo = load(1, wo_h, wo)
-    c_x = load(2, x_h, x_v)
+    c_x = load(2, x_h, du)
     c_cot = load(3, cot_h, cot)
     c_w = [
         (
@@ -301,7 +447,6 @@
     c_n1 = load(n0 + 1, n1_h, n1)
     c_wk = load(n0 + 2, wk_h, wk)
     c_wv = load(n0 + 3, wv_h, wv)
-    c_wq = load(n0 + 4, wq_h, wq)
 
     def e_copy(t, slot):
         return pltpu.make_async_copy(e_h.at[t], e_v.at[slot], esem.at[slot])
@@ -312,21 +457,22 @@
     gain1, shift1 = vec[0:1, :], vec[1:2, :]
     b_out, gain2, shift2, b_down = vec[4:5, :], vec[5:6, :], vec[6:7, :], vec[7:8, :]
     sm[...] = jnp.zeros_like(sm)
-    for c in (c_a, c_wo, c_x, c_cot):
-        c.wait()
+    for w in (c_a, c_wo, c_x, c_cot):
+        w.wait()
 
     def first(i, _):
         r = pl.ds(al(i * R), R)
-        h = x_v[r, :].astype(f32) + dg(a_v[r, :], wo[...], NN) + b_out
+        h = du[r, :].astype(f32) + dg(a_v[r, :], wo[...], NN) + b_out
         h_v[r, :] = h
-        z, _r = row_norm(h)
-        n2[r, :] = (z * gain2 + shift2).astype(bf16)
+        zn, _r = row_norm(h)
+        n2[r, :] = (zn * gain2 + shift2).astype(bf16)
         acc[r, :] = h + b_down
         dn2[r, :] = jnp.zeros((R, D), f32)
         sm[7:8, :] += jnp.sum(cot[r, :].astype(f32), axis=0, keepdims=True)
         return 0
 
     lax.fori_loop(0, C, first, 0)
+    pl.semaphore_wait(bar, len(beside))
 
     def ffn(j, _):
         jr = pl.ds(al(j * D), D)
@@ -355,8 +501,23 @@
             dn2[r, :] += dg(d, vv[jr, :], NT)
             return sums + jnp.sum(d.astype(f32), axis=0, keepdims=True)
 
-        sm[pl.ds(8 + j, 1), :] = lax.fori_loop(0, C, chunk, jnp.zeros((1, D), f32))
+        dj = lax.fori_loop(0, C, chunk, jnp.zeros((1, D), f32))
+        sm[pl.ds(8 + j, 1), :] = dj
+
+        @pl.when(j >= 3)
+        def _():
+            step4(j - 3)
+
+        @pl.when(j >= 2)
+        def _():
+            step3(j - 2)
+
+        @pl.when(j >= 1)
+        def _():
+            step2(j - 1, True)
+
         gb[j] = dg(n2[...], du[...], TN).astype(bf16).reshape(B // 2, 2, CH, D)
+        step1(j, False)
         gw = dg(pb[...], cot[...], TN).astype(bf16)
         per = FF // B
         for bb in range(D // per):
@@ -366,6 +527,8 @@
         return 0
 
     lax.fori_loop(0, J, ffn, 0)
+    for u in (J, J + 1, J + 2):
+        step1(u, True)
 
     c_k = load(0, k_h, kk.at[pl.ds(0, t_rows)])
     c_v = load(1, v_h, vv.at[pl.ds(0, t_rows)])
@@ -373,15 +536,15 @@
     def second(i, _):
         r = pl.ds(al(i * R), R)
         pb[r, :] = acc[r, :].astype(bf16)
-        z, rr = row_norm(h_v[r, :])
-        dn = dn2[r, :]
-        g = dn * gain2
-        sm[5:6, :] += jnp.sum(dn * z, axis=0, keepdims=True)
-        sm[6:7, :] += jnp.sum(dn, axis=0, keepdims=True)
+        zn, rr = row_norm(h_v[r, :])
+        dnn = dn2[r, :]
+        g = dnn * gain2
+        sm[5:6, :] += jnp.sum(dnn * zn, axis=0, keepdims=True)
+        sm[6:7, :] += jnp.sum(dnn, axis=0, keepdims=True)
         dh = cot[r, :].astype(f32) + rr * (
             g
             - jnp.mean(g, axis=-1, keepdims=True)
-            - z * jnp.mean(g * z, axis=-1, keepdims=True)
+            - zn * jnp.mean(g * zn, axis=-1, keepdims=True)
         )
         h_v[r, :] = dh
         db = dh.astype(bf16)
@@ -394,12 +557,18 @@
     c_li = load(2, li_h, acc)
     c_o = pltpu.make_async_copy(pb, out_h, osem.at[0])
     c_o.start()
-    c_dh = pltpu.make_async_copy(h_v, dh_h, osem.at[1])
-    c_dh.start()
-    gb[2 * J] = dg(a_v[...], n2[...], TN).astype(bf16).reshape(B // 2, 2, CH, D)
-
-    for c in (c_k, c_v, c_li, c_q, c_wk, c_wv, c_wq, c_n1):
-        c.wait()
+    step5(0)
+    step4(1)
+    step3(2)
+    step2(3, True)
+    step1(J + 3, True)
+    sent(0)
+    c_wq = load(3, wq_h, wo)
+    gb[slot(2 * J)] = dg(a_v[...], n2[...], TN).astype(bf16).reshape(B // 2, 2, CH, D)
+
+    c_x = load(4, x_h, n2)
+    for w in (c_o, c_x, c_k, c_v, c_li, c_q, c_wk, c_wv, c_wq, c_n1):
+        w.wait()
     dq_v, do_v = cot, du
     lane = lax.broadcasted_iota(jnp.int32, (1, 128), 1)
     lo = lane < 64
@@ -428,51 +597,164 @@
         kk[rk, lanes] = (dg(qs, ds, TN) * (1.0 / LOG2E)).astype(bf16).T
         vv[rk, lanes] = dg(dos, e_v[slot], TN).astype(bf16).T
 
+        third = t // 3
+        hit = t % 3 == 0
+
+        @pl.when(t == 1)
+        def _():
+            step3(3)
+            step4(2)
+            step5(1)
+            step1(2 * J, True)
+
+        @pl.when(t == 4)
+        def _():
+            step4(3)
+            step5(2)
+
+        @pl.when(t == 7)
+        def _():
+            step5(3)
+
+        @pl.when(hit & (t >= 6))
+        def _():
+            step4(J + third - 2)
+
+        @pl.when(hit & (t >= 3))
+        def _():
+            step3(J + third - 1)
+
+        @pl.when(hit & (t <= 9))
+        def _():
+            step2(J + third, True)
+
+        @pl.when(t == 12)
+        def _():
+            cp5(0).wait_recv()
+            step2(2 * J, False)
+
+        @pl.when((t % 3 == 2) & (t >= 8))
+        def _():
+            step5(J + third - 2)
+
+        for i in range(C - 1):
+
+            @pl.when(t == (i + 1) * pairs + 3)
+            def _():
+                rows2(i)
+
+        @pl.when(t == pairs + 8)
+        def _():
+            rows3(0)
+
         @pl.when(t + 2 < C * pairs)
         def _():
             e_copy(t + 2, slot).start()
 
         @pl.when(p == pairs - 1)
         def _():
+            @pl.when(q == 2)
+            def _():
+                for i in range(4):
+                    dcp(0, i).wait_send()
+
             def block(i, _):
                 blk = (s + 1 + i) % S
                 rr = pl.ds(al((q * S + blk) * R), R)
                 f = dg(kk[rr, :], wk[...], NT) + dg(vv[rr, :], wv[...], NT)
-                f += jnp.where(blk == s, 1.0, 0.0) * dg(dq_v[rq, :], wq[...], NT)
+                f += jnp.where(blk == s, 1.0, 0.0) * dg(dq_v[rq, :], wo[...], NT)
                 n = n1[rr, :].astype(f32)
                 sm[0:1, :] += jnp.sum(f * n, axis=0, keepdims=True)
                 sm[1:2, :] += jnp.sum(f, axis=0, keepdims=True)
-                dn[rr, :] = f.astype(bf16)
+                dn[q % 2, blk // 2, blk % 2] = f.astype(bf16)
                 return 0
 
             lax.fori_loop(0, S, block, 0)
+            rows1(q)
 
         return 0
 
     lax.fori_loop(0, C * pairs, pair, 0)
-    c_dn = pltpu.make_async_copy(dn, dn_h, osem.at[2])
-    c_dn.start()
-    sm[0:1, :] = (sm[0:1, :] - shift1 * sm[1:2, :]) / gain1
+    step4(2 * J)
+    for u in (1, 2, 3):
+        sent(u)
+        cp5(u).wait_recv()
     sm[2:3, :] = jnp.sum(dq_v[...].astype(f32), axis=0, keepdims=True)
     sm[3:4, :] = jnp.sum(vv[0:t_rows, :].astype(f32), axis=0, keepdims=True)
+    sm[0:1, :] = (sm[0:1, :] - shift1 * sm[1:2, :]) / gain1
+
+    def mcp(i, src, dst, dev):
+        return remote(src, dst, ms.at[i], mr.at[i], dev)
+
+    m1 = mcp(0, sm, mc.at[0], (s, sib))
+    m1.start()
     for i in range(C):
         r = pl.ds(i * R, R)
-        x_v[r, :] = n1[pl.ds(al((i * S + s) * R), R), :]
-    gb[2 * J + 1] = dg(x_v[...], dq_v[...], TN).astype(bf16).reshape(B // 2, 2, CH, D)
-    gb[2 * J + 2] = dg(n1[...], kk[0:t_rows, :], TN).astype(bf16).reshape(B // 2, 2, CH, D)
-    gb[2 * J + 3] = dg(n1[...], vv[0:t_rows, :], TN).astype(bf16).reshape(B // 2, 2, CH, D)
-    c_g = pltpu.make_async_copy(gb, g_h, osem.at[3])
-    c_g.start()
-    c_s = pltpu.make_async_copy(sm, sm_h, osem.at[4])
+        a_v[r, :] = n1[pl.ds(al((i * S + s) * R), R), :]
+    gb[slot(2 * J + 1)] = dg(a_v[...], dq_v[...], TN).astype(bf16).reshape(B // 2, 2, CH, D)
+    step1(2 * J + 1, True)
+    rows2(2)
+    gb[slot(2 * J + 2)] = dg(n1[...], kk[0:t_rows, :], TN).astype(bf16).reshape(B // 2, 2, CH, D)
+    step1(2 * J + 2, True)
+    step2(2 * J + 1, False)
+    step5(2 * J)
+    m1.wait()
+    mz[0] = sm[...] + mc[0]
+    m2 = [mcp(k, mz.at[0], mz.at[k], (s, (z + k) % 4 * 2 + c)) for k in (1, 2, 3)]
+    for m in m2:
+        m.start()
+    rows3(1)
+    gb[slot(2 * J + 3)] = dg(n1[...], vv[0:t_rows, :], TN).astype(bf16).reshape(B // 2, 2, CH, D)
+    step1(2 * J + 3, True)
+    step3(2 * J + 1)
+    step2(2 * J + 2, False)
+    for m in m2:
+        m.wait()
+    mx[0] = (mz[0] + mz[1]) + (mz[2] + mz[3])
+    m3 = mcp(4, mx.at[0], mx.at[1], (px, b))
+    m3.start()
+    rows3(2)
+    c_i = pltpu.make_async_copy(pb, ig_h, osem.at[1])
+    c_i.start()
+    step2(2 * J + 3, False)
+    m3.wait()
+    mx[2] = mx[0] + mx[1]
+    m4 = mcp(5, mx.at[2], mx.at[3], (py, b))
+    m4.start()
+    step3(2 * J + 2)
+    step4(2 * J + 1)
+    step3(2 * J + 3)
+    step4(2 * J + 2)
+    step5(2 * J + 1)
+    m4.wait()
+    sm[...] = mx[2] + mx[3]
+    c_s = pltpu.make_async_copy(sm, sm_h, osem.at[2])
     c_s.start()
-    for c in (c_o, c_dh, c_dn, c_g, c_s):
-        c.wait()
+    step4(2 * J + 3)
+    step5(2 * J + 2)
+    step5(2 * J + 3)
+    for u in range(U):
+        if u > 3:
+            cp5(u).wait_recv()
+    c_f = pltpu.make_async_copy(f, f_h, osem.at[3])
+    c_f.start()
+    for u in range(U):
+        if u > 3:
+            sent(u)
+        if u >= 2 * J:
+            cp4(u).wait_send()
+        cp5(u).wait_send()
+    for q in (1, 2):
+        for i in range(4):
+            dcp(q, i).wait_send()
+    for o in (c_i, c_s, c_f):
+        o.wait()
 
 
 def backward(C, R, D, S, FF, x, cot, a, li, q, k, v, n1, e, vec, bup, wo, wu, wd, wq, wk, wv):
     N, T = C * R, R * S
     J = FF // D
-    U = 2 * J + 4
+    U, CH = 2 * J + 4, D // 8
     sd = jax.ShapeDtypeStruct
     dma = pltpu.SemaphoreType.DMA
     vm = pltpu.VMEM
@@ -480,24 +762,32 @@
         functools.partial(backward_kernel, C, R, D, S, FF),
         out_shape=(
             sd((N, D), bf16),
-            sd((N, D), f32),
-            sd((U, 4, 2, D // 8, D), bf16),
-            sd((C * T, D), bf16),
+            sd((N, D), bf16),
+            sd((U, D // 8, D), bf16),
             sd((16, D), f32),
         ),
         in_specs=[ANY] * 9 + [VM, VM] + [ANY] * 6,
-        out_specs=(ANY,) * 5,
+        out_specs=(ANY,) * 4,
         scratch_shapes=[
-            vm((N, D), bf16), vm((N, D), bf16), vm((N, D), bf16), vm((N, D), bf16),
+            vm((N, D), bf16), vm((N, D), bf16), vm((N, D), bf16),
             vm((N, D), bf16), vm((N, D), bf16), vm((N, D), bf16),
             vm((N, D), f32), vm((N, D), f32), vm((N, D), f32),
             vm((FF, D), bf16), vm((FF, D), bf16), vm((C * T, D), bf16),
-            vm((D, D), bf16), vm((D, D), bf16), vm((D, D), bf16), vm((D, D), bf16),
-            vm((U, 4, 2, D // 8, D), bf16), vm((C * T, D), bf16),
+            vm((D, D), bf16), vm((D, D), bf16), vm((D, D), bf16),
+            vm((2 * J, 4, 2, CH, D), bf16), vm((2, 2, 2, R, D), bf16),
             vm((2, 2 * R, T), bf16), vm((16, D), f32),
-            dma((4 + 2 * J + 5,)), dma((2,)), dma((5,)),
+            vm((4, 4, CH, D), bf16), vm((2 * J, 4, CH // 2, D), bf16), vm((U, 3, CH // 2, D), bf16),
+            vm((4, CH // 2, D), bf16), vm((U, CH // 2, D), bf16), vm((U, CH, D), bf16),
+            vm((2, 2, 2, R // 2, D), bf16), vm((C, 2, R // 2, D), bf16),
+            vm((1, 16, D), f32), vm((4, 16, D), f32), vm((4, 16, D), f32),
+            dma((4 + 2 * J + 4,)), dma((2,)), dma((4,)),
+            dma((4, U)), dma((4, U)), dma((3, U)), dma((3, U)),
+            dma((4, C)), dma((4, C)), dma((6,)), dma((6,)),
+            pltpu.SemaphoreType.REGULAR((4,)),
         ],
-        compiler_params=pltpu.CompilerParams(vmem_limit_bytes=62 * 2**20),
+        compiler_params=pltpu.CompilerParams(
+            collective_id=2, has_side_effects=True, vmem_limit_bytes=(64 * 2**20) - 2**17
+        ),
         cost_estimate=pl.CostEstimate(
             flops=40 * 10**9, bytes_accessed=60 * 10**6, transcendentals=0
         ),
@@ -519,26 +809,14 @@
     ).astype(f32)
     bup = b_up.reshape(FF // D, D).astype(f32)
     n1, q, k, v, a, li, e = attend(C, R, D, S, x, lengths, vec, w_query, w_key, w_value)
-    out, dh, g, dn, sm = backward(
+    out, input_grad, g, sm = backward(
         C, R, D, S, FF, x, cot, a, li, q, k, v, n1, e, vec, bup, w_out, w_up, w_down,
         w_query, w_key, w_value,
     )
-    dn = lax.psum_scatter(
-        dn.reshape(C, S, R, D), "seq", scatter_dimension=1, tiled=True
-    ).reshape(N, D).astype(f32)
-    z, r = row_norm(x.astype(f32))
-    gg = dn * gain_one.astype(f32)
-    dx = r * (
-        gg - jnp.mean(gg, axis=-1, keepdims=True) - z * jnp.mean(gg * z, axis=-1, keepdims=True)
-    )
-    input_grad = (dh + dx).astype(bf16)
-    sm = lax.psum(sm, ("seq", "batch"))
     b = lax.axis_index("batch")
-    U = g.shape[0]
-    g = lax.psum_scatter(g.reshape(U, 8, D // 8, D), "batch", scatter_dimension=1, tiled=True)
-    g = lax.psum(g, "seq").reshape(U, D // 8, D).astype(f32)
     J = FF // D
     part = D // 8
+    g = g.astype(f32)
     small = lax.dynamic_slice(sm, (0, b * part), (8, part))
     up = jnp.concatenate([g[i] for i in range(J)], axis=1)
     down = g[J : 2 * J].reshape(FF // 8, D)

time: 524 us -> 231 us (0.44)
  waiting for transfers between devices: 295 us -> 0 us
  Pallas kernels: 141 us -> 213 us
  blocking collectives: 40.7 us -> 0 us
  between operations: 15.6 us -> 0.7 us
  local copies, waits for them, and re-layouts: 20.7 us -> 13.5 us
  other arithmetic: 9.57 us -> 3.54 us
    unnamed x5 -> x0, waiting for transfers between devices: 279 us -> none
    pallas_call x1, Pallas kernels: 83.3 us -> 155 us  [backward(): pl.pallas_call(functools.partial(backward_kernel, C, R, D, S, FF), out_sh...]
    psum x1 -> x0, blocking collectives: 40.7 us -> none  [fast_body(): sm = lax.psum(sm, ('seq', 'batch'))]
    psum x1 -> x0, waiting for transfers between devices: 16.4 us -> none  [fast_body(): g = lax.psum(g, 'seq').reshape(U, D // 8, D).astype(f32)]
  transfers between devices with their start and end apart: 3 -> 0, of which waited for: 2 -> 0; matrix products, arithmetic and copies ran while one was open for 3% -> 0% of each run, Pallas kernels for 0% -> 0%
where the time goes in v2:
time: 231 us; the launch traced here: 230 us
  Pallas kernels  213 us (92%)
  local copies, waits for them, and re-layouts  13.5 us (6%)
  other arithmetic  3.54 us (2%)
    pallas_call x1, Pallas kernels, backward(): pl.pallas_call(functools.partial(backward_kernel, C, R, D, S, FF), out_sh...  155 us
    pallas_call x1, Pallas kernels, attend(): pl.pallas_call(functools.partial(attend_kernel, C, R, D, S), out_shape=(s...  57.9 us
    another operation x9, local copies, waits for them, and re-layouts, fast_body(): jnp.stack((gain_one, shift_one, b_query, b_value, b_out, gain_two, shift_...  5.53 us

profile of v2, /device:TPU:0, one launch (start us, length us, event | category | flops | bytes accessed | tf_op | source)
XLA Modules:
  0.0 230.4 jit_solution(8165714498355524241)
XLA Ops:
  0.7 0.7 stack.27
  1.3 0.7 stack.28
  2.0 0.7 stack.29
  2.7 0.7 stack.30
  3.4 0.7 stack.31
  4.1 0.7 stack.32
  4.8 0.7 stack.33
  5.5 0.7 stack.34
  6.2 0.6 convert_element_type.11.vec
  6.8 57.9 %shard_map.305 = (bf16[2688,768]{1,0:T(8,128)(2,1)}, bf16[672,768]{1,0:T(8,128)(2,1)}, bf16[2688,768]{1,0:T(8,128)(2,1)}, bf16[2688,768]{1,0:T(8,128)(2,1)}, bf1...) custom-call(bf16[672,768]{1,0:T(8,128)(2,1)} %bitcast.40, s32[3]{0:T(128)} %len_s.1, ...), custom_call_target="tpu_custom_call" | custom-call | flops 20000000000 | bytes 40000000 | tf_op jit(solution)/shard_map/pallas_call | solution.py:229
  64.7 0.6 reshape.61.bup
  65.3 154.7 %shard_map.306 = (bf16[672,768]{1,0:T(8,128)(2,1)}, bf16[672,768]{1,0:T(8,128)(2,1)}, bf16[12,96,768]{2,1,0:T(8,128)(2,1)}, f32[16,768]{1,0:T(8,128)}) custom-call(bf16[672,768]{1,0:T(8,128)(2,1)} %bitcast.41, bf16[672,768]{1,0:T(8,128)(2,1)} %bitcast.42, bf16[672,768]{1,0:T(8,128)(2,1)} %get-tuple-element.28.a_h, f32[672,768]{1,0:T(8,128)} %get-tuple-element.29.li_h, ...), custom_call_target="tpu_custom_call" | custom-call | flops 40000000000 | bytes 60000000 | tf_op jit(solution)/shard_map/pallas_call | solution.py:761
  220.1 1.8 convert_element_type.14
  221.9 1.1 slice_bitcast_fusion.3
  222.9 1.1 pad_maximum_fusion
  224.1 0.8 constant_dynamic-slice_fusion
  224.8 0.5 slice_bitcast_fusion.8
  225.4 0.7 slice.69
  226.1 0.7 dynamic_slice.7
  226.8 0.0 copy-done
  226.8 1.1 slice.80
  227.9 0.5 copy-done.2
  228.4 1.0 copy.37
  229.4 1.0 copy.38
  (8 shorter events, 0.1 us)
Async XLA Ops:
  6.8 57.9 %copy-start.3 = (bf16[3072]{0:T(1024)(128)(2,1)S(1)}, bf16[3072]{0:T(1024)(128)(2,1)}, u32[]{:S(2)}) copy-start(bf16[3072]{0:T(1024)(128)(2,1)} %param.32) | copy-start | bytes 18436
  222.9 3.9 %copy-start = (bf16[12,96,768]{2,1,0:T(8,128)(2,1)S(1)}, bf16[12,96,768]{2,1,0:T(8,128)(2,1)}, u32[]{:S(2)}) copy-start(bf16[12,96,768]{2,1,0:T(8,128)(2,1)} %get-tuple-element.38) | copy-start | bytes 5308420
  226.8 1.6 copy-start.2
  227.9 1.5 copy-start.1

commit v3 on v2

--- a/solution.py
+++ b/solution.py
@@ -30,6 +30,10 @@
     return lax.dot_general(a, b, dims, preferred_element_type=f32)
 
 
+def row(ref):
+    return ref[...].astype(f32).reshape(1, ref.shape[0])
+
+
 def al(i, m=16):
     return pl.multiple_of(i, m)
 
@@ -50,10 +54,10 @@
 
 def attend_kernel(
     C, R, D, S,
-    x_h, len_s, vec, wq_h, wk_h, wv_h,
-    n1_h, q_h, k_h, v_h, a_h, li_h, e_h,
-    x_v, n1, wq, wk, wv, q_v, k_v, v_v, a_v, li_v, e_v, s_v,
-    lsem, osem, esem, sx, sy, rx, ry, sdx, sdy, rdx, rdy,
+    x_h, cot_h, len_s, g_r, s_r, bq_r, bv_r, wq_h, wk_h, wv_h, wd_h,
+    n1_h, q_h, k_h, v_h, a_h, li_h, e_h, gu_h,
+    x_v, n1, wq, wk, wv, q_v, k_v, v_v, a_v, li_v, e_v, s_v, cot, wd, gu,
+    lsem, osem, esem, gsem, os, orr, rs, rr,
 ):
     T = R * S
     HR = R // 2
@@ -72,7 +76,7 @@
         c.start()
     wc = [
         pltpu.make_async_copy(h, v, lsem.at[C + i])
-        for i, (h, v) in enumerate(((wk_h, wk), (wv_h, wv), (wq_h, wq)))
+        for i, (h, v) in enumerate(((wk_h, wk), (wv_h, wv), (wq_h, wq), (cot_h, cot), (wd_h, wd)))
     ]
     for c in wc:
         c.start()
@@ -80,26 +84,28 @@
     def rows(q, blk, off, n):
         return pl.ds(al((q * S + blk) * R + off), n)
 
-    def own_copy(q, peer, ss, rs):
-        ref = n1.at[rows(q, s, 0, R)]
-        return pltpu.make_async_remote_copy(
-            ref, ref, ss.at[q], rs.at[q], device_id=(peer, b), device_id_type=MESH
-        )
-
-    def relay_copy(q, peer, blk, off, ss, rs):
+    def copy(q, peer, blk, off, ss, rs):
         ref = n1.at[rows(q, blk, off, HR)]
         return pltpu.make_async_remote_copy(
-            ref, ref, ss.at[q], rs.at[q], device_id=(peer, b), device_id_type=MESH
-        )
-
-    own = [(own_copy(q, px, sx, rx), own_copy(q, py, sy, ry)) for q in range(C)]
-    rel = [
-        (relay_copy(q, py, px, 0, sdy, rdy), relay_copy(q, px, py, HR, sdx, rdx))
+            ref, ref, ss, rs, device_id=(peer, b), device_id_type=MESH
+        )
+
+    own = [
+        [
+            copy(q, peer, s, off, os.at[i, q], orr.at[i, q])
+            for i, (peer, off) in enumerate(((px, 0), (py, HR), (px, HR), (py, 0)))
+        ]
         for q in range(C)
     ]
-
-    gain, shift = vec[0:1, :], vec[1:2, :]
-    bq, bv = vec[2:3, :], vec[3:4, :]
+    rel = [
+        [
+            copy(q, peer, blk, off, rs.at[i, q], rr.at[i, q])
+            for i, (peer, blk, off) in enumerate(((py, px, 0), (px, py, HR)))
+        ]
+        for q in range(C)
+    ]
+
+    gain, shift, bq, bv = (row(r) for r in (g_r, s_r, bq_r, bv_r))
     for q in range(C):
         xc[q].wait()
         z, _ = row_norm(x_v[q * R : (q + 1) * R, :].astype(f32))
@@ -109,7 +115,7 @@
         if q < 2:
             for c in own[q]:
                 c.start()
-    for c in wc:
+    for c in wc[:3]:
         c.wait()
 
     def kv(q, blk):
@@ -130,14 +136,30 @@
     qc = pltpu.make_async_copy(q_v, q_h, osem.at[0])
     qc.start()
 
-    def arrived(q):
-        for c in own[q]:
+    def onward(q):
+        for c in own[q][:2]:
             c.wait_recv()
         for c in rel[q]:
             c.start()
 
     def near(q):
+        for c in own[q][2:]:
+            c.wait_recv()
         lax.fori_loop(0, 2, lambda i, c: (kv(q, jnp.where(i == 0, px, py)), c)[1], 0)
+
+    def gu_copy(j):
+        return pltpu.make_async_copy(
+            gu.at[pl.ds(al(j * C * R), C * R)], gu_h.at[pl.ds(al(j * C * R), C * R)], gsem.at[j]
+        )
+
+    def hidden(j, _):
+        gu[pl.ds(al(j * C * R), C * R), :] = dg(
+            cot[...], wd[pl.ds(al(j * D), D), :], NT
+        ).astype(bf16)
+        gu_copy(j).start()
+        return 0
+
+    J = wd.shape[0] // D
 
     def far(q):
         for c in rel[q]:
@@ -148,11 +170,15 @@
                 v.at[pl.ds(q * T, T)], h.at[pl.ds(q * T, T)], osem.at[3 + 3 * q + i]
             ).start()
 
-    arrived(0)
+    onward(0)
+    for c in wc[3:]:
+        c.wait()
+    lax.fori_loop(0, J // 2, hidden, 0)
+    near(0)
+    lax.fori_loop(J // 2, J, hidden, 0)
+    onward(1)
     for c in own[2]:
         c.start()
-    near(0)
-    arrived(1)
     near(1)
     far(0)
 
@@ -166,16 +192,15 @@
     def pair(t, _):
         q, p = t // pairs, t % pairs
 
-        @pl.when(t == pairs // 2)
+        @pl.when(t == pairs)
         def _():
-            arrived(2)
+            far(1)
+            onward(2)
+
+        @pl.when(t == 2 * pairs)
+        def _():
             near(2)
-
-        for i in range(1, C):
-
-            @pl.when(t == i * pairs)
-            def _():
-                far(i)
+            far(2)
 
         off = al(p * 128, 128)
         rq = pl.ds(al(q * R), R)
@@ -217,12 +242,14 @@
             ).wait()
         for c in own[q] + rel[q]:
             c.wait_send()
+    for j in range(J):
+        gu_copy(j).wait()
     qc.wait()
     ac.wait()
     lc.wait()
 
 
-def attend(C, R, D, S, x, lengths, vec, wq, wk, wv):
+def attend(C, R, D, S, FF, x, cot, lengths, vecs, wq, wk, wv, wd):
     N, T, pairs = C * R, R * S, D // 128
     sd = jax.ShapeDtypeStruct
     dma = pltpu.SemaphoreType.DMA
@@ -236,9 +263,10 @@
             sd((N, D), bf16),
             sd((N, D), f32),
             sd((C * pairs, 2 * R, T), bf16),
+            sd((FF // D * N, D), bf16),
         ),
-        in_specs=[ANY, SM, VM, ANY, ANY, ANY],
-        out_specs=(ANY,) * 7,
+        in_specs=[ANY, ANY, SM] + [VM] * 4 + [ANY] * 4,
+        out_specs=(ANY,) * 8,
         scratch_shapes=[
             pltpu.VMEM((N, D), bf16),
             pltpu.VMEM((C * T, D), bf16),
@@ -252,27 +280,66 @@
             pltpu.VMEM((N, D), f32),
             pltpu.VMEM((2, 2 * R, T), bf16),
             pltpu.VMEM((2 * R, T), f32),
-            dma((C + 3,)),
+            pltpu.VMEM((N, D), bf16),
+            pltpu.VMEM((FF, D), bf16),
+            pltpu.VMEM((FF // D * N, D), bf16),
+            dma((C + 5,)),
             dma((3 + 3 * C,)),
             dma((2,)),
-        ]
-        + [dma((C,))] * 8,
+            dma((FF // D,)),
+            dma((4, C)),
+            dma((4, C)),
+            dma((2, C)),
+            dma((2, C)),
+        ],
         compiler_params=pltpu.CompilerParams(
             collective_id=1, has_side_effects=True, vmem_limit_bytes=60 * 2**20
         ),
         cost_estimate=pl.CostEstimate(
             flops=20 * 10**9, bytes_accessed=40 * 10**6, transcendentals=0
         ),
-    )(x, lengths, vec, wq, wk, wv)
+    )(x, cot, lengths, *vecs, wq, wk, wv, wd)
+
+
+SCHEDULE = {
+    "w1": ((2, 0),),
+    "f30": ((2, 1),),
+    "u3": ((3, 0),),
+    "w3": ((2, 2),),
+    "s0": ((2, 3),),
+    "s1": ((1, 4),),
+    "s2": ((3, 1), (1, 7),),
+    "wo": ((1, 6), (2, 4), (1, 5), (4, 0),),
+    "t0": ((2, 7), (3, 2),),
+    "t1": ((1, 8),),
+    "t3": ((5, 0), (2, 5), (3, 3), (4, 1), (2, 8),),
+    "t6": ((3, 7), (6, 0), (5, 1),),
+    "t9": ((3, 4),),
+    "t11": ((4, 3),),
+    "d12": ((4, 2), (3, 5),),
+    "d13": ((7, 0),),
+    "t12": ((6, 1), (2, 6),),
+    "t16": ((4, 4), (8, 0),),
+    "t17": ((5, 2),),
+    "d21": ((5, 3),),
+    "k": ((1, 9), (3, 8), (4, 5), (7, 1), (2, 9),),
+    "v": ((1, 10), (3, 6),),
+    "o0": ((5, 5), (1, 11), (2, 10), (2, 11), (3, 9), (6, 2),),
+    "o1": ((5, 4), (4, 6), (4, 7), (4, 8), (3, 10), (4, 9), (3, 11), (7, 2), (5, 6),),
+    "o2": ((4, 10), (5, 7), (4, 11),),
+    "end0": ((5, 8), (5, 9),),
+    "end1": ((5, 10), (5, 11), (8, 2), (8, 1),),
+}
 
 
 def backward_kernel(
     C, R, D, S, FF,
-    x_h, cot_h, a_h, li_h, q_h, k_h, v_h, n1_h, e_h, vec, bup, wo_h, wu_h, wd_h, wq_h, wk_h, wv_h,
-    out_h, ig_h, f_h, sm_h,
+    x_h, cot_h, a_h, li_h, q_h, k_h, v_h, n1_h, e_h, gu_h,
+    g1_r, s1_r, bo_r, g2_r, s2_r, bd_r, bu_r, wo_h, wu_h, wd_h, wq_h, wk_h, wv_h,
+    out_h, ig_h, f_h, sm_h, p_h,
     cot, a_v, q_v, n2, pb, du, h_v, acc, dn2, kk, vv, n1, wk, wv, wo, gb, dn, e_v, sm,
-    rc, r2, r3, s3, r4, f, d1, d2, mc, mz, mx,
-    lsem, esem, osem, sems, rems, zs, zr, ds_s, ds_r, ms, mr, cr,
+    rc, r2, r3, s3, r4, f, d1, d2, mc, mz, mx, bup,
+    lsem, esem, osem, psem, sems, rems, zs, zr, ds_s, ds_r, ms, mr, cr,
 ):
     T, N = R * S, C * R
     pairs = D // 128
@@ -426,6 +493,25 @@
             ).astype(bf16)
 
 
+    def emit(name):
+        for k, u in SCHEDULE.get(name, ()):
+            if k == 1:
+                step1(u, True)
+            elif k == 2:
+                if u >= 2 * J:
+                    if u == 2 * J:
+                        cp5(0).wait_recv()
+                    step2(u, False)
+                else:
+                    step2(u, True)
+            else:
+                {3: step3, 4: step4, 5: step5, 6: rows1, 7: rows2, 8: rows3}[k](u)
+
+    def emit_when(names):
+        for name, cond in names:
+            if name in SCHEDULE:
+                pl.when(cond)(functools.partial(emit, name))
+
     def load(i, h, v):
         cp = pltpu.make_async_copy(h, v, lsem.at[i])
         cp.start()
@@ -435,10 +521,22 @@
     c_wo = load(1, wo_h, wo)
     c_x = load(2, x_h, du)
     c_cot = load(3, cot_h, cot)
+    def e_copy(t, slot):
+        return pltpu.make_async_copy(e_h.at[t], e_v.at[slot], esem.at[slot])
+
+
+    gain1, shift1, b_out, gain2, shift2, b_down = (
+        row(r) for r in (g1_r, s1_r, bo_r, g2_r, s2_r, bd_r)
+    )
+    for j in range(J):
+        bup[j : j + 1, :] = bu_r[j * D : (j + 1) * D].astype(f32).reshape(1, D)
+    sm[...] = jnp.zeros_like(sm)
+    for w in (c_a, c_wo, c_x, c_cot):
+        w.wait()
     c_w = [
         (
             load(4 + 2 * j, wu_h.at[:, pl.ds(j * D, D)], vv.at[pl.ds(j * D, D)]),
-            load(5 + 2 * j, wd_h.at[pl.ds(j * D, D)], kk.at[pl.ds(j * D, D)]),
+            load(5 + 2 * j, gu_h.at[pl.ds(j * N, N)], kk.at[pl.ds(j * N, N)]),
         )
         for j in range(J)
     ]
@@ -447,18 +545,8 @@
     c_n1 = load(n0 + 1, n1_h, n1)
     c_wk = load(n0 + 2, wk_h, wk)
     c_wv = load(n0 + 3, wv_h, wv)
-
-    def e_copy(t, slot):
-        return pltpu.make_async_copy(e_h.at[t], e_v.at[slot], esem.at[slot])
-
     e_copy(0, 0).start()
     e_copy(1, 1).start()
-
-    gain1, shift1 = vec[0:1, :], vec[1:2, :]
-    b_out, gain2, shift2, b_down = vec[4:5, :], vec[5:6, :], vec[6:7, :], vec[7:8, :]
-    sm[...] = jnp.zeros_like(sm)
-    for w in (c_a, c_wo, c_x, c_cot):
-        w.wait()
 
     def first(i, _):
         r = pl.ds(al(i * R), R)
@@ -474,6 +562,11 @@
     lax.fori_loop(0, C, first, 0)
     pl.semaphore_wait(bar, len(beside))
 
+    def p_copy(j):
+        return pltpu.make_async_copy(
+            kk.at[pl.ds(al(j * N), N)], p_h.at[pl.ds(al(j * N), N)], psem.at[j]
+        )
+
     def ffn(j, _):
         jr = pl.ds(al(j * D), D)
         for jj in range(J):
@@ -486,56 +579,50 @@
         bias = bup[pl.ds(j, 1), :]
 
         def chunk(i, sums):
+            emit_when(
+                (f"f{jj}{ii}", (j == jj) & (i == ii)) for jj in range(J) for ii in range(C)
+            )
             r = pl.ds(al(i * R), R)
             u = dg(n2[r, :], vv[jr, :], NN) + bias
-            g = dg(cot[r, :], kk[jr, :], NT)
+            rj = pl.ds(al(j * N + i * R), R)
+            g = kk[rj, :].astype(f32)
             u2 = u * u
             t = jnp.tanh(u * (GC0 + GC1 * u2))
             hu = 0.5 * u
             half = 0.5 + 0.5 * t
             p = (u * half).astype(bf16)
             d = (g * (half + hu * (1.0 - t * t) * (GC0 + 3.0 * GC1 * u2))).astype(bf16)
-            pb[r, :] = p
+            kk[rj, :] = p
             du[r, :] = d
-            acc[r, :] += dg(p, kk[jr, :], NN)
             dn2[r, :] += dg(d, vv[jr, :], NT)
             return sums + jnp.sum(d.astype(f32), axis=0, keepdims=True)
 
         dj = lax.fori_loop(0, C, chunk, jnp.zeros((1, D), f32))
         sm[pl.ds(8 + j, 1), :] = dj
-
-        @pl.when(j >= 3)
-        def _():
-            step4(j - 3)
-
-        @pl.when(j >= 2)
-        def _():
-            step3(j - 2)
-
-        @pl.when(j >= 1)
-        def _():
-            step2(j - 1, True)
-
+        emit_when((f"u{jj}", j == jj) for jj in range(J))
         gb[j] = dg(n2[...], du[...], TN).astype(bf16).reshape(B // 2, 2, CH, D)
         step1(j, False)
-        gw = dg(pb[...], cot[...], TN).astype(bf16)
+        emit_when((f"w{jj}", j == jj) for jj in range(J))
         per = FF // B
+        pt = kk.at[pl.ds(al(j * N), N)]
         for bb in range(D // per):
+            gw = dg(pt[:, bb * per : (bb + 1) * per], cot[...], TN).astype(bf16)
             for i in range(per // CH):
-                o = bb * per + i * CH
-                gb[J + i, j, bb] = gw[o : o + CH, :]
+                gb[J + i, j, bb] = gw[i * CH : (i + 1) * CH, :]
+        p_copy(j).start()
         return 0
 
     lax.fori_loop(0, J, ffn, 0)
-    for u in (J, J + 1, J + 2):
-        step1(u, True)
-
+
+    c_v = load(1, v_h, vv.at[pl.ds(0, t_rows)])
+
+    for j in range(J):
+        p_copy(j).wait()
     c_k = load(0, k_h, kk.at[pl.ds(0, t_rows)])
-    c_v = load(1, v_h, vv.at[pl.ds(0, t_rows)])
 
     def second(i, _):
+        emit_when((f"s{ii}", i == ii) for ii in range(C))
         r = pl.ds(al(i * R), R)
-        pb[r, :] = acc[r, :].astype(bf16)
         zn, rr = row_norm(h_v[r, :])
         dnn = dn2[r, :]
         g = dnn * gain2
@@ -554,20 +641,15 @@
         return 0
 
     lax.fori_loop(0, C, second, 0)
-    c_li = load(2, li_h, acc)
-    c_o = pltpu.make_async_copy(pb, out_h, osem.at[0])
-    c_o.start()
-    step5(0)
-    step4(1)
-    step3(2)
-    step2(3, True)
-    step1(J + 3, True)
+    c_li = load(2, li_h, dn2)
+    emit("wo")
     sent(0)
     c_wq = load(3, wq_h, wo)
     gb[slot(2 * J)] = dg(a_v[...], n2[...], TN).astype(bf16).reshape(B // 2, 2, CH, D)
 
     c_x = load(4, x_h, n2)
-    for w in (c_o, c_x, c_k, c_v, c_li, c_q, c_wk, c_wv, c_wq, c_n1):
+    emit("kw")
+    for w in (c_x, c_k, c_v, c_li, c_q, c_wk, c_wv, c_wq, c_n1):
         w.wait()
     dq_v, do_v = cot, du
     lane = lax.broadcasted_iota(jnp.int32, (1, 128), 1)
@@ -580,11 +662,12 @@
     def pair(t, _):
         q, p = t // pairs, t % pairs
         slot = t % 2
+        emit_when((f"t{tt}", t == tt) for tt in range(C * pairs))
         lanes = pl.ds(al(p * 128, 128), 128)
         rq = pl.ds(al(q * R), R)
         rk = pl.ds(al(q * T), T)
         qs = stack(q_v[rq, lanes])
-        dof = do_v[rq, lanes].astype(f32) * acc[rq, lanes]
+        dof = do_v[rq, lanes].astype(f32) * dn2[rq, lanes]
         dos = stack(dof.astype(bf16))
         dl = jnp.sum(stack(dof * a_v[rq, lanes].astype(f32)), axis=1, keepdims=True)
         e_copy(t, slot).wait()
@@ -597,56 +680,6 @@
         kk[rk, lanes] = (dg(qs, ds, TN) * (1.0 / LOG2E)).astype(bf16).T
         vv[rk, lanes] = dg(dos, e_v[slot], TN).astype(bf16).T
 
-        third = t // 3
-        hit = t % 3 == 0
-
-        @pl.when(t == 1)
-        def _():
-            step3(3)
-            step4(2)
-            step5(1)
-            step1(2 * J, True)
-
-        @pl.when(t == 4)
-        def _():
-            step4(3)
-            step5(2)
-
-        @pl.when(t == 7)
-        def _():
-            step5(3)
-
-        @pl.when(hit & (t >= 6))
-        def _():
-            step4(J + third - 2)
-
-        @pl.when(hit & (t >= 3))
-        def _():
-            step3(J + third - 1)
-
-        @pl.when(hit & (t <= 9))
-        def _():
-            step2(J + third, True)
-
-        @pl.when(t == 12)
-        def _():
-            cp5(0).wait_recv()
-            step2(2 * J, False)
-
-        @pl.when((t % 3 == 2) & (t >= 8))
-        def _():
-            step5(J + third - 2)
-
-        for i in range(C - 1):
-
-            @pl.when(t == (i + 1) * pairs + 3)
-            def _():
-                rows2(i)
-
-        @pl.when(t == pairs + 8)
-        def _():
-            rows3(0)
-
         @pl.when(t + 2 < C * pairs)
         def _():
             e_copy(t + 2, slot).start()
@@ -658,27 +691,39 @@
                 for i in range(4):
                     dcp(0, i).wait_send()
 
-            def block(i, _):
-                blk = (s + 1 + i) % S
+            def put(blk, more):
                 rr = pl.ds(al((q * S + blk) * R), R)
-                f = dg(kk[rr, :], wk[...], NT) + dg(vv[rr, :], wv[...], NT)
-                f += jnp.where(blk == s, 1.0, 0.0) * dg(dq_v[rq, :], wo[...], NT)
+                d = dg(kk[rr, :], wk[...], NT) + dg(vv[rr, :], wv[...], NT)
+                if more:
+                    d += dg(dq_v[rq, :], wo[...], NT)
                 n = n1[rr, :].astype(f32)
-                sm[0:1, :] += jnp.sum(f * n, axis=0, keepdims=True)
-                sm[1:2, :] += jnp.sum(f, axis=0, keepdims=True)
-                dn[q % 2, blk // 2, blk % 2] = f.astype(bf16)
+                sm[0:1, :] += jnp.sum(d * n, axis=0, keepdims=True)
+                sm[1:2, :] += jnp.sum(d, axis=0, keepdims=True)
+                dn[q % 2, blk // 2, blk % 2] = d.astype(bf16)
+
+            def others(i, _):
+                emit_when(
+                    (f"d{qq}{ii}", (q == qq) & (i == ii)) for qq in range(C) for ii in range(S - 1)
+                )
+                put((s + 1 + i) % S, False)
                 return 0
 
-            lax.fori_loop(0, S, block, 0)
-            rows1(q)
+            lax.fori_loop(0, S - 1, others, 0)
+            emit_when((f"d{qq}{S - 1}", q == qq) for qq in range(C))
+            put(s, True)
 
         return 0
 
     lax.fori_loop(0, C * pairs, pair, 0)
-    step4(2 * J)
     for u in (1, 2, 3):
         sent(u)
         cp5(u).wait_recv()
+    for i in range(C):
+        r = pl.ds(i * R, R)
+        a_v[r, :] = n1[pl.ds(al((i * S + s) * R), R), :]
+    q_u, k_u, v_u = 2 * J + 1, 2 * J + 2, 2 * J + 3
+    emit("q")
+    gb[slot(q_u)] = dg(a_v[...], dq_v[...], TN).astype(bf16).reshape(B // 2, 2, CH, D)
     sm[2:3, :] = jnp.sum(dq_v[...].astype(f32), axis=0, keepdims=True)
     sm[3:4, :] = jnp.sum(vv[0:t_rows, :].astype(f32), axis=0, keepdims=True)
     sm[0:1, :] = (sm[0:1, :] - shift1 * sm[1:2, :]) / gain1
@@ -688,51 +733,63 @@
 
     m1 = mcp(0, sm, mc.at[0], (s, sib))
     m1.start()
-    for i in range(C):
-        r = pl.ds(i * R, R)
-        a_v[r, :] = n1[pl.ds(al((i * S + s) * R), R), :]
-    gb[slot(2 * J + 1)] = dg(a_v[...], dq_v[...], TN).astype(bf16).reshape(B // 2, 2, CH, D)
-    step1(2 * J + 1, True)
-    rows2(2)
-    gb[slot(2 * J + 2)] = dg(n1[...], kk[0:t_rows, :], TN).astype(bf16).reshape(B // 2, 2, CH, D)
-    step1(2 * J + 2, True)
-    step2(2 * J + 1, False)
-    step5(2 * J)
+    emit("k")
+    for i in range(2):
+        gb[slot(k_u), 2 * i : 2 * i + 2] = (
+            dg(n1[:, i * (D // 2) : (i + 1) * (D // 2)], kk[0:t_rows, :], TN)
+            .astype(bf16)
+            .reshape(2, 2, CH, D)
+        )
     m1.wait()
     mz[0] = sm[...] + mc[0]
     m2 = [mcp(k, mz.at[0], mz.at[k], (s, (z + k) % 4 * 2 + c)) for k in (1, 2, 3)]
     for m in m2:
         m.start()
-    rows3(1)
-    gb[slot(2 * J + 3)] = dg(n1[...], vv[0:t_rows, :], TN).astype(bf16).reshape(B // 2, 2, CH, D)
-    step1(2 * J + 3, True)
-    step3(2 * J + 1)
-    step2(2 * J + 2, False)
+    c_wd = load(0, wd_h, kk)
+    emit("v")
+    for i in range(2):
+        gb[slot(v_u), 2 * i : 2 * i + 2] = (
+            dg(n1[:, i * (D // 2) : (i + 1) * (D // 2)], vv[0:t_rows, :], TN)
+            .astype(bf16)
+            .reshape(2, 2, CH, D)
+        )
+    c_p = load(1, p_h, n1)
+    emit("o0")
+    c_wd.wait()
+    c_p.wait()
+
+    def last(i):
+        r = pl.ds(al(i * R), R)
+        o = acc[r, :]
+        for j in range(J):
+            o += dg(n1[pl.ds(al(j * N + i * R), R), :], kk[j * D : (j + 1) * D, :], NN)
+        q_v[r, :] = o.astype(bf16)
+
+    last(0)
+    emit("o1")
     for m in m2:
         m.wait()
     mx[0] = (mz[0] + mz[1]) + (mz[2] + mz[3])
     m3 = mcp(4, mx.at[0], mx.at[1], (px, b))
     m3.start()
-    rows3(2)
-    c_i = pltpu.make_async_copy(pb, ig_h, osem.at[1])
-    c_i.start()
-    step2(2 * J + 3, False)
+    last(1)
+    emit("o2")
     m3.wait()
     mx[2] = mx[0] + mx[1]
     m4 = mcp(5, mx.at[2], mx.at[3], (py, b))
     m4.start()
-    step3(2 * J + 2)
-    step4(2 * J + 1)
-    step3(2 * J + 3)
-    step4(2 * J + 2)
-    step5(2 * J + 1)
+    last(2)
+    c_o = pltpu.make_async_copy(q_v, out_h, osem.at[0])
+    c_o.start()
+    emit("end0")
     m4.wait()
     sm[...] = mx[2] + mx[3]
     c_s = pltpu.make_async_copy(sm, sm_h, osem.at[2])
     c_s.start()
-    step4(2 * J + 3)
-    step5(2 * J + 2)
-    step5(2 * J + 3)
+    emit("end1")
+    c_i = pltpu.make_async_copy(pb, ig_h, osem.at[1])
+    c_i.start()
+    emit("end2")
     for u in range(U):
         if u > 3:
             cp5(u).wait_recv()
@@ -747,11 +804,11 @@
     for q in (1, 2):
         for i in range(4):
             dcp(q, i).wait_send()
-    for o in (c_i, c_s, c_f):
+    for o in (c_o, c_i, c_s, c_f):
         o.wait()
 
 
-def backward(C, R, D, S, FF, x, cot, a, li, q, k, v, n1, e, vec, bup, wo, wu, wd, wq, wk, wv):
+def backward(C, R, D, S, FF, x, cot, a, li, q, k, v, n1, e, gu, vecs, wo, wu, wd, wq, wk, wv):
     N, T = C * R, R * S
     J = FF // D
     U, CH = 2 * J + 4, D // 8
@@ -765,9 +822,10 @@
             sd((N, D), bf16),
             sd((U, D // 8, D), bf16),
             sd((16, D), f32),
+            sd((J * N, D), bf16),
         ),
-        in_specs=[ANY] * 9 + [VM, VM] + [ANY] * 6,
-        out_specs=(ANY,) * 4,
+        in_specs=[ANY] * 10 + [VM] * 7 + [ANY] * 6,
+        out_specs=(ANY,) * 5,
         scratch_shapes=[
             vm((N, D), bf16), vm((N, D), bf16), vm((N, D), bf16),
             vm((N, D), bf16), vm((N, D), bf16), vm((N, D), bf16),
@@ -779,8 +837,8 @@
             vm((4, 4, CH, D), bf16), vm((2 * J, 4, CH // 2, D), bf16), vm((U, 3, CH // 2, D), bf16),
             vm((4, CH // 2, D), bf16), vm((U, CH // 2, D), bf16), vm((U, CH, D), bf16),
             vm((2, 2, 2, R // 2, D), bf16), vm((C, 2, R // 2, D), bf16),
-            vm((1, 16, D), f32), vm((4, 16, D), f32), vm((4, 16, D), f32),
-            dma((4 + 2 * J + 4,)), dma((2,)), dma((4,)),
+            vm((1, 16, D), f32), vm((4, 16, D), f32), vm((4, 16, D), f32), vm((J, D), f32),
+            dma((4 + 2 * J + 4,)), dma((2,)), dma((4,)), dma((J,)),
             dma((4, U)), dma((4, U)), dma((3, U)), dma((3, U)),
             dma((4, C)), dma((4, C)), dma((6,)), dma((6,)),
             pltpu.SemaphoreType.REGULAR((4,)),
@@ -791,7 +849,59 @@
         cost_estimate=pl.CostEstimate(
             flops=40 * 10**9, bytes_accessed=60 * 10**6, transcendentals=0
         ),
-    )(x, cot, a, li, q, k, v, n1, e, vec, bup, wo, wu, wd, wq, wk, wv)
+    )(x, cot, a, li, q, k, v, n1, e, gu, *vecs, wo, wu, wd, wq, wk, wv)
+
+
+def finish_kernel(D, FF, f_h, sm, out_h, ig_h, *rest):
+    o_out, o_ig, g1, s1, wq, bq, wk, wv, bv, wo, bo, g2, s2, wu, bu, wd, bd, f, v_out, v_ig, sem = rest
+    J, CH = FF // D, D // 8
+    c1 = pltpu.make_async_copy(f_h, f, sem.at[0])
+    c2 = pltpu.make_async_copy(out_h, v_out, sem.at[1])
+    c3 = pltpu.make_async_copy(ig_h, v_ig, sem.at[2])
+    for c in (c1, c2, c3):
+        c.start()
+    b = lax.axis_index("batch")
+    c2.wait()
+    c4 = pltpu.make_async_copy(v_out, o_out, sem.at[1])
+    c4.start()
+    c3.wait()
+    c5 = pltpu.make_async_copy(v_ig, o_ig, sem.at[2])
+    c5.start()
+    rolled = pltpu.roll(sm[0:8, :], (8 - b) % 8 * CH, 1)
+    for i, o in enumerate((g1, s1, bq, bv, bo, g2, s2, bd)):
+        o[...] = rolled[i, :CH]
+    per = FF // 8
+    half = D // per
+    up = sm[8 : 8 + J, :]
+    here = lax.broadcasted_iota(jnp.int32, (J, 1), 0) == b // half
+    up = jnp.sum(jnp.where(here, up, 0.0), axis=0, keepdims=True)
+    up = jnp.where(b % half == 0, up[:, :per], up[:, per:])
+    bu[...] = up[0]
+    c1.wait()
+    for j in range(J):
+        wu[:, j * D : (j + 1) * D] = f[j].astype(f32)
+        wd[j * CH : (j + 1) * CH, :] = f[J + j].astype(f32)
+    for i, o in enumerate((wo, wq, wk, wv)):
+        o[...] = f[2 * J + i].astype(f32)
+    c4.wait()
+    c5.wait()
+
+
+def finish(D, FF, f, sm, out, ig):
+    sd = jax.ShapeDtypeStruct
+    CH = D // 8
+    row, mat = sd((CH,), f32), sd((CH, D), f32)
+    return pl.pallas_call(
+        functools.partial(finish_kernel, D, FF),
+        out_shape=(
+            sd(out.shape, bf16), sd(ig.shape, bf16), row, row, mat, row, mat, mat, row, mat,
+            row, row, row, sd((CH, FF), f32), sd((FF // 8,), f32), sd((FF // 8, D), f32), row,
+        ),
+        in_specs=[ANY, VM, ANY, ANY],
+        out_specs=(ANY, ANY) + (VM,) * 15,
+        scratch_shapes=[pltpu.VMEM(v.shape, bf16) for v in (f, out, ig)] + [pltpu.SemaphoreType.DMA((3,))],
+        compiler_params=pltpu.CompilerParams(vmem_limit_bytes=62 * 2**20),
+    )(f, sm, out, ig)
 
 
 def fast_body(
@@ -804,28 +914,17 @@
     N = C * R
     x = inputs.reshape(N, D)
     cot = cotangent.reshape(N, D)
-    vec = jnp.stack(
-        (gain_one, shift_one, b_query, b_value, b_out, gain_two, shift_two, b_down)
-    ).astype(f32)
-    bup = b_up.reshape(FF // D, D).astype(f32)
-    n1, q, k, v, a, li, e = attend(C, R, D, S, x, lengths, vec, w_query, w_key, w_value)
-    out, input_grad, g, sm = backward(
-        C, R, D, S, FF, x, cot, a, li, q, k, v, n1, e, vec, bup, w_out, w_up, w_down,
-        w_query, w_key, w_value,
+    n1, q, k, v, a, li, e, gu = attend(
+        C, R, D, S, FF, x, cot, lengths, (gain_one, shift_one, b_query, b_value),
+        w_query, w_key, w_value, w_down,
     )
-    b = lax.axis_index("batch")
-    J = FF // D
-    part = D // 8
-    g = g.astype(f32)
-    small = lax.dynamic_slice(sm, (0, b * part), (8, part))
-    up = jnp.concatenate([g[i] for i in range(J)], axis=1)
-    down = g[J : 2 * J].reshape(FF // 8, D)
-    gbup = lax.dynamic_slice(sm[8 : 8 + J].reshape(FF), (b * (FF // 8),), (FF // 8,))
-    return (
-        out.reshape(inputs.shape), input_grad.reshape(inputs.shape),
-        small[0], small[1], g[2 * J + 1], small[2], g[2 * J + 2], g[2 * J + 3], small[3],
-        g[2 * J], small[4], small[5], small[6], up, gbup, down, small[7],
+    out, input_grad, g, sm, _ = backward(
+        C, R, D, S, FF, x, cot, a, li, q, k, v, n1, e, gu,
+        (gain_one, shift_one, b_out, gain_two, shift_two, b_down, b_up),
+        w_out, w_up, w_down, w_query, w_key, w_value,
     )
+    out, input_grad, *grads = finish(D, FF, g, sm, out, input_grad)
+    return (out.reshape(inputs.shape), input_grad.reshape(inputs.shape), *grads)
 
 
 def from_behind(x, axis, by):

time: 231 us -> 192 us (0.83)
  Pallas kernels: 213 us -> 191 us
  local copies, waits for them, and re-layouts: 13.5 us -> 0 us
  other arithmetic: 3.54 us -> 0 us
    pallas_call x1, Pallas kernels: 155 us -> 129 us  [backward(): pl.pallas_call(functools.partial(backward_kernel, C, R, D, S, FF), out_sh...]
    pallas_call x0 -> x1, Pallas kernels: none -> 5.7 us  [finish(): pl.pallas_call(functools.partial(finish_kernel, D, FF), out_shape=(sd(out...]
    another operation x9 -> x0, local copies, waits for them, and re-layouts: 5.53 us -> none  [fast_body(): jnp.stack((gain_one, shift_one, b_query, b_value, b_out, gain_two, shift_...]
    pallas_call x1, Pallas kernels: 57.9 us -> 55.4 us  [attend(): pl.pallas_call(functools.partial(attend_kernel, C, R, D, S), out_shape=(s...]
    unnamed x10 -> x0, local copies, waits for them, and re-layouts: 2.47 us -> none
    convert_element_type x2 -> x0, other arithmetic: 2.41 us -> none  [the longest x1 1.8 us: fast_body(): g = g.astype(f32)]
where the time goes in v3:
time: 192 us; the launch traced here: 191 us
  Pallas kernels  191 us (99%)
    pallas_call x1, Pallas kernels, backward(): pl.pallas_call(functools.partial(backward_kernel, C, R, D, S, FF), out_sh...  129 us
    pallas_call x1, Pallas kernels, attend(): pl.pallas_call(functools.partial(attend_kernel, C, R, D, S), out_shape=(s...  55.4 us
    pallas_call x1, Pallas kernels, finish(): pl.pallas_call(functools.partial(finish_kernel, D, FF), out_shape=(sd(out...  5.7 us

profile of v3, /device:TPU:0, one launch (start us, length us, event | category | flops | bytes accessed | tf_op | source)
XLA Modules:
  0.0 191.4 jit_solution(1462557578410654513)
XLA Ops:
  0.7 55.4 %shard_map.305 = (bf16[2688,768]{1,0:T(8,128)(2,1)}, bf16[672,768]{1,0:T(8,128)(2,1)}, bf16[2688,768]{1,0:T(8,128)(2,1)}, bf16[2688,768]{1,0:T(8,128)(2,1)}, bf1...) custom-call(bf16[672,768]{1,0:T(8,128)(2,1)} %bitcast.4, ...), custom_call_target="tpu_custom_call" | custom-call | flops 20000000000 | bytes 40000000 | tf_op jit(solution)/shard_map/pallas_call | solution.py:256
  56.1 129.4 %shard_map.306 = (bf16[672,768]{1,0:T(8,128)(2,1)}, bf16[672,768]{1,0:T(8,128)(2,1)}, bf16[12,96,768]{2,1,0:T(8,128)(2,1)}, f32[16,768]{1,0:T(8,128)}, bf16[2688,768]{1,0:T(8,128)(2,1)}) custom-call(bf16[672,768]{1,0:T(8,128)(2,1)} %bitcast.5, bf16[672,768]{1,0:T(8,128)(2,1)} %bitcast.7, bf16[672,768]{1,0:T(8,128)(2,1)} %get-tuple-element.46.a_h, ...), custom_call_target="tpu_custom_call" | custom-call | flops 40000000000 | bytes 60000000 | tf_op jit(solution)/shard_map/pallas_call | solution.py:818
  185.5 5.7 %shard_map.307 = (bf16[672,768]{1,0:T(8,128)(2,1)}, bf16[672,768]{1,0:T(8,128)(2,1)}, f32[96]{0:T(128)}, f32[96]{0:T(128)}, f32[96,768]{1,0:T(8,128)}, /*index=5...) custom-call(bf16[12,96,768]{2,1,0:T(8,128)(2,1)} %get-tuple-element., ...), custom_call_target="tpu_custom_call" | custom-call | tf_op jit(solution)/shard_map/pallas_call | solution.py:894

commit v4 on v3

--- a/solution.py
+++ b/solution.py
@@ -186,55 +186,72 @@
     lo = lane < 64
     col = lax.broadcasted_iota(jnp.int32, (1, T), 1)
 
-    def e_copy(t):
-        return pltpu.make_async_copy(e_v.at[t % 2], e_h.at[t], esem.at[t % 2])
-
-    def pair(t, _):
+    def e_copy(t, slot):
+        return pltpu.make_async_copy(e_v.at[slot], e_h.at[t], esem.at[slot])
+
+    def scores(t):
         q, p = t // pairs, t % pairs
-
-        @pl.when(t == pairs)
+        lanes = pl.ds(al(p * 128, 128), 128)
+        qp = q_v[pl.ds(al(q * R), R), lanes]
+        zero = jnp.zeros_like(qp)
+        qs = jnp.concatenate([jnp.where(lo, qp, zero), jnp.where(lo, zero, qp)], 0)
+        bias = jnp.where(col < len_s[q], 0.0, masked_score).astype(f32)
+        return dg(qs, k_v[pl.ds(al(q * T), T), lanes], NT) + bias
+
+    def weigh(t, slot):
+        q, p = t // pairs, t % pairs
+        lanes = pl.ds(al(p * 128, 128), 128)
+        rq = pl.ds(al(q * R), R)
+        m = jnp.max(s_v[slot], axis=1, keepdims=True)
+        e = jnp.exp2(s_v[slot] - m)
+        eb = e.astype(bf16)
+        tot = jnp.sum(e, axis=1, keepdims=True)
+        e_v[slot] = eb
+        ol = dg(eb, v_v[pl.ds(al(q * T), T), lanes], NN)
+        inv = 1.0 / tot
+        inv = jnp.where(lo, inv[:R], inv[R:])
+        li_v[rq, lanes] = inv
+        a_v[rq, lanes] = (jnp.where(lo, ol[:R], ol[R:]) * inv).astype(bf16)
+
+    def sequence(q, _):
+        @pl.when(q == 1)
         def _():
             far(1)
             onward(2)
 
-        @pl.when(t == 2 * pairs)
+        @pl.when(q == 2)
         def _():
             near(2)
             far(2)
 
-        off = al(p * 128, 128)
-        rq = pl.ds(al(q * R), R)
-        rk = pl.ds(al(q * T), T)
-        qp = q_v[rq, pl.ds(off, 128)]
-        zero = jnp.zeros_like(qp)
-        qs = jnp.concatenate([jnp.where(lo, qp, zero), jnp.where(lo, zero, qp)], 0)
-        bias = jnp.where(col < len_s[q], 0.0, masked_score).astype(f32)
-        s_v[...] = dg(qs, k_v[rk, pl.ds(off, 128)], NT) + bias
-        m = jnp.max(s_v[...], axis=1, keepdims=True)
-        e = jnp.exp2(s_v[...] - m)
-        eb = e.astype(bf16)
-        tot = jnp.sum(e, axis=1, keepdims=True)
-
-        @pl.when(t >= 2)
-        def _():
-            e_copy(t - 2).wait()
-
-        e_v[t % 2] = eb
-        e_copy(t).start()
-        ol = dg(eb, v_v[rk, pl.ds(off, 128)], NN)
-        inv = 1.0 / tot
-        inv = jnp.where(lo, inv[:R], inv[R:])
-        li_v[rq, pl.ds(off, 128)] = inv
-        a_v[rq, pl.ds(off, 128)] = (jnp.where(lo, ol[:R], ol[R:]) * inv).astype(bf16)
+        s_v[0] = scores(q * pairs)
+
+        def two(h, _):
+            t = q * pairs + 2 * h
+
+            @pl.when(t >= 2)
+            def _():
+                e_copy(t - 2, 0).wait()
+                e_copy(t - 1, 1).wait()
+
+            s_v[1] = scores(t + 1)
+            weigh(t, 0)
+            s_v[0] = scores(q * pairs + lax.rem(2 * h + 2, pairs))
+            weigh(t + 1, 1)
+            e_copy(t, 0).start()
+            e_copy(t + 1, 1).start()
+            return 0
+
+        lax.fori_loop(0, pairs // 2, two, 0)
         return 0
 
-    lax.fori_loop(0, C * pairs, pair, 0)
+    lax.fori_loop(0, C, sequence, 0)
     ac = pltpu.make_async_copy(a_v, a_h, osem.at[1])
     lc = pltpu.make_async_copy(li_v, li_h, osem.at[2])
     ac.start()
     lc.start()
-    e_copy(C * pairs - 2).wait()
-    e_copy(C * pairs - 1).wait()
+    e_copy(C * pairs - 2, 0).wait()
+    e_copy(C * pairs - 1, 1).wait()
     for q in range(C):
         for i, (v, h) in enumerate(((n1, n1_h), (k_v, k_h), (v_v, v_h))):
             pltpu.make_async_copy(
@@ -279,7 +296,7 @@
             pltpu.VMEM((N, D), bf16),
             pltpu.VMEM((N, D), f32),
             pltpu.VMEM((2, 2 * R, T), bf16),
-            pltpu.VMEM((2 * R, T), f32),
+            pltpu.VMEM((2, 2 * R, T), f32),
             pltpu.VMEM((N, D), bf16),
             pltpu.VMEM((FF, D), bf16),
             pltpu.VMEM((FF // D * N, D), bf16),
@@ -302,33 +319,39 @@
 
 
 SCHEDULE = {
-    "w1": ((2, 0),),
-    "f30": ((2, 1),),
-    "u3": ((3, 0),),
-    "w3": ((2, 2),),
-    "s0": ((2, 3),),
-    "s1": ((1, 4),),
-    "s2": ((3, 1), (1, 7),),
-    "wo": ((1, 6), (2, 4), (1, 5), (4, 0),),
-    "t0": ((2, 7), (3, 2),),
-    "t1": ((1, 8),),
-    "t3": ((5, 0), (2, 5), (3, 3), (4, 1), (2, 8),),
-    "t6": ((3, 7), (6, 0), (5, 1),),
-    "t9": ((3, 4),),
-    "t11": ((4, 3),),
-    "d12": ((4, 2), (3, 5),),
-    "d13": ((7, 0),),
-    "t12": ((6, 1), (2, 6),),
-    "t16": ((4, 4), (8, 0),),
-    "t17": ((5, 2),),
-    "d21": ((5, 3),),
-    "k": ((1, 9), (3, 8), (4, 5), (7, 1), (2, 9),),
-    "v": ((1, 10), (3, 6),),
-    "o0": ((5, 5), (1, 11), (2, 10), (2, 11), (3, 9), (6, 2),),
-    "o1": ((5, 4), (4, 6), (4, 7), (4, 8), (3, 10), (4, 9), (3, 11), (7, 2), (5, 6),),
-    "o2": ((4, 10), (5, 7), (4, 11),),
-    "end0": ((5, 8), (5, 9),),
-    "end1": ((5, 10), (5, 11), (8, 2), (8, 1),),
+    "f11": ((1, 4),),
+    "f12": ((2, 0),),
+    "w1": ((2, 4),),
+    "f21": ((1, 5),),
+    "f22": ((2, 1),),
+    "f30": ((3, 0),),
+    "u3": ((2, 2),),
+    "w3": ((2, 5),),
+    "s0": ((3, 1),),
+    "s1": ((2, 3),),
+    "s2": ((1, 6), (4, 0),),
+    "t0": ((2, 6), (3, 2),),
+    "t1": ((1, 7),),
+    "t3": ((4, 1),),
+    "t4": ((3, 3),),
+    "t5": ((2, 7),),
+    "d00": ((5, 1), (5, 0),),
+    "t6": ((6, 0), (10, 3), (10, 1), (10, 0), (10, 2), (3, 4),),
+    "t8": ((1, 8),),
+    "t11": ((4, 2), (2, 8),),
+    "d11": ((4, 4), (3, 5),),
+    "d12": ((4, 3), (7, 0),),
+    "t12": ((6, 1), (3, 6),),
+    "t16": ((5, 3),),
+    "q": ((5, 2),),
+    "k": ((1, 9), (3, 8), (4, 5), (4, 6), (3, 7), (2, 9),),
+    "v": ((1, 10), (7, 1),),
+    "d20": ((2, 10), (5, 6), (1, 11), (5, 4), (8, 0), (3, 9), (2, 11),),
+    "o0": ((6, 2), (3, 10),),
+    "o1": ((3, 11), (4, 8), (5, 5), (4, 7), (4, 10), (4, 9), (7, 2),),
+    "o2": ((5, 7), (8, 1), (4, 11), (5, 10), (5, 9), (5, 8),),
+    "end0": ((8, 2),),
+    "end2": ((5, 11),),
 }
 
 
@@ -337,9 +360,9 @@
     x_h, cot_h, a_h, li_h, q_h, k_h, v_h, n1_h, e_h, gu_h,
     g1_r, s1_r, bo_r, g2_r, s2_r, bd_r, bu_r, wo_h, wu_h, wd_h, wq_h, wk_h, wv_h,
     out_h, ig_h, f_h, sm_h, p_h,
-    cot, a_v, q_v, n2, pb, du, h_v, acc, dn2, kk, vv, n1, wk, wv, wo, gb, dn, e_v, sm,
+    cot, a_v, q_v, n2, du, h_v, acc, dn2, kk, vv, n1, wk, wv, wo, gb, dn, e_v, sm,
     rc, r2, r3, s3, r4, f, d1, d2, mc, mz, mx, bup,
-    lsem, esem, osem, psem, sems, rems, zs, zr, ds_s, ds_r, ms, mr, cr,
+    lsem, esem, osem, psem, tsem, trem, sems, rems, zs, zr, ds_s, ds_r, ms, mr, cr,
 ):
     T, N = R * S, C * R
     pairs = D // 128
@@ -363,23 +386,60 @@
             src, dst, ss, rs, device_id=dev, device_id_type=MESH
         )
 
+    def axis(u):
+        return (u - J) // (J // 2) if J <= u < 2 * J else u % 2
+
+    def down(u):
+        return isinstance(u, int) and J <= u < 2 * J
+
+    def rslot(u):
+        if not isinstance(u, int) or u < J:
+            return u
+        return J if u < 2 * J else u - 2 * J
+
     def slot(u):
         return u - 2 * J * (u // (2 * J))
 
     def mine(u):
-        return x + (u % 2) * (y - x)
+        return (x, y)[axis(u)]
 
     def first_peer(u):
-        return px + (u % 2) * (py - px)
+        return (px, py)[axis(u)]
 
     def last_peer(u):
-        return py + (u % 2) * (px - py)
+        return (py, px)[axis(u)]
 
     def half(h):
         return pl.ds(al(h * HC), HC)
 
     def cp1(u):
-        return remote(gb.at[slot(u), :, 1 - c], rc.at[u % 4], sems.at[0, u], rems.at[0, u], (s, sib))
+        part = gb.at[pl.ds(J, J), u - J, 1 - c] if down(u) else gb.at[slot(u), :, 1 - c]
+        return remote(part, rc.at[rslot(u)], sems.at[0, u], rems.at[0, u], (s, sib))
+
+    def tile_copies(j):
+        ux, uy = pl.ds(J, J // 2), pl.ds(J + J // 2, J // 2)
+        return (
+            remote(
+                gb.at[ux, j, c, half(1 - x)], r2.at[ux, j], sems.at[1, J + j], rems.at[1, J + j],
+                (px, b),
+            ),
+            remote(gb.at[uy, j, c, half(1 - y)], r2.at[uy, j], tsem.at[j], trem.at[j], (py, b)),
+        )
+
+    def tile2(j):
+        cp1(J + j).wait_recv()
+        gb[J : 2 * J, j, c] += rc[rslot(J + j)]
+        if j < J - 1:
+            pl.semaphore_signal(cr.at[rslot(J + j)], 1, device_id=(s, sib), device_id_type=MESH)
+        for o in tile_copies(j):
+            o.start()
+
+    def tile3(j):
+        for o in tile_copies(j):
+            o.wait_recv()
+        mid = J + J // 2
+        gb[J:mid, j, c, half(x)] += r2[J:mid, j]
+        gb[mid : 2 * J, j, c, half(y)] += r2[mid : 2 * J, j]
 
     def cp2(u):
         return remote(
@@ -403,25 +463,27 @@
 
     def sent(u):
         cp1(u).wait_send()
-        cp2(u).wait_send()
+        for o in tile_copies(u - J) if down(u) else (cp2(u),):
+            o.wait_send()
         for k in (1, 2, 3):
             cp3(u, k).wait_send()
 
     def step1(u, again):
         if again:
-            pl.semaphore_wait(cr.at[u % 4], 1)
+            pl.semaphore_wait(cr.at[rslot(u)], 1)
         cp1(u).start()
 
     def step2(u, more):
         cp1(u).wait_recv()
-        gb[slot(u), :, c] += rc[u % 4]
+        gb[slot(u), :, c] += rc[rslot(u)]
         if more:
-            pl.semaphore_signal(cr.at[u % 4], 1, device_id=(s, sib), device_id_type=MESH)
+            pl.semaphore_signal(cr.at[rslot(u)], 1, device_id=(s, sib), device_id_type=MESH)
         cp2(u).start()
 
     def step3(u):
-        cp2(u).wait_recv()
-        gb[slot(u), :, c, half(mine(u))] += r2[slot(u)]
+        if not down(u):
+            cp2(u).wait_recv()
+            gb[slot(u), :, c, half(mine(u))] += r2[slot(u)]
         for k in (1, 2, 3):
             cp3(u, k).start()
 
@@ -455,9 +517,9 @@
         elif i == 1:
             a, o, dev = dn.at[sl, 1 - y, :, pl.ds(HR, HR)], d1.at[sl, 1], py
         elif i == 2:
-            a, o, dev = dn.at[sl, 1 - y, x, pl.ds(0, HR)], d2.at[q, 0], py
+            a, o, dev = dn.at[sl, 1 - y, x, pl.ds(0, HR)], d2.at[sl, 0], py
         else:
-            a, o, dev = dn.at[sl, y, 1 - x, pl.ds(HR, HR)], d2.at[q, 1], px
+            a, o, dev = dn.at[sl, y, 1 - x, pl.ds(HR, HR)], d2.at[sl, 1], px
         return remote(a, o, ds_s.at[i, q], ds_r.at[i, q], (dev, b))
 
     def rows1(q):
@@ -478,11 +540,11 @@
         dcp(q, 2).wait_recv()
         dcp(q, 3).wait_recv()
         for i in range(2):
-            d = dn[sl, y, x, i * HR : (i + 1) * HR].astype(f32) + d2[q, i].astype(f32)
+            d = dn[sl, y, x, i * HR : (i + 1) * HR].astype(f32) + d2[sl, i].astype(f32)
             r = pl.ds(al(q * R + i * HR), HR)
             zz, rr = row_norm(n2[r, :].astype(f32))
             g = d * gain1
-            pb[r, :] = (
+            du[r, :] = (
                 h_v[r, :]
                 + rr
                 * (
@@ -496,7 +558,9 @@
     def emit(name):
         for k, u in SCHEDULE.get(name, ()):
             if k == 1:
-                step1(u, True)
+                step1(u, u > J)
+            elif k == 2 and down(u):
+                tile2(u - J)
             elif k == 2:
                 if u >= 2 * J:
                     if u == 2 * J:
@@ -505,12 +569,22 @@
                 else:
                     step2(u, True)
             else:
-                {3: step3, 4: step4, 5: step5, 6: rows1, 7: rows2, 8: rows3}[k](u)
+                {3: step3, 4: step4, 5: step5, 6: rows1, 7: rows2, 8: rows3, 10: tile3}[k](u)
 
     def emit_when(names):
         for name, cond in names:
             if name in SCHEDULE:
                 pl.when(cond)(functools.partial(emit, name))
+
+    def weight(u, left, right):
+        def part(i, _):
+            lanes = pl.ds(al(i * (D // 2), 128), D // 2)
+            gb[slot(u), pl.ds(2 * i, 2)] = (
+                dg(left[:, lanes], right[...], TN).astype(bf16).reshape(2, 2, CH, D)
+            )
+            return 0
+
+        lax.fori_loop(0, 2, part, 0)
 
     def load(i, h, v):
         cp = pltpu.make_async_copy(h, v, lsem.at[i])
@@ -600,15 +674,19 @@
         dj = lax.fori_loop(0, C, chunk, jnp.zeros((1, D), f32))
         sm[pl.ds(8 + j, 1), :] = dj
         emit_when((f"u{jj}", j == jj) for jj in range(J))
-        gb[j] = dg(n2[...], du[...], TN).astype(bf16).reshape(B // 2, 2, CH, D)
+        weight(j, n2, du)
         step1(j, False)
         emit_when((f"w{jj}", j == jj) for jj in range(J))
         per = FF // B
         pt = kk.at[pl.ds(al(j * N), N)]
-        for bb in range(D // per):
-            gw = dg(pt[:, bb * per : (bb + 1) * per], cot[...], TN).astype(bf16)
+
+        def rows_of(bb, _):
+            gw = dg(pt[:, pl.ds(al(bb * per, 128), per)], cot[...], TN).astype(bf16)
             for i in range(per // CH):
                 gb[J + i, j, bb] = gw[i * CH : (i + 1) * CH, :]
+            return 0
+
+        lax.fori_loop(0, D // per, rows_of, 0)
         p_copy(j).start()
         return 0
 
@@ -645,7 +723,7 @@
     emit("wo")
     sent(0)
     c_wq = load(3, wq_h, wo)
-    gb[slot(2 * J)] = dg(a_v[...], n2[...], TN).astype(bf16).reshape(B // 2, 2, CH, D)
+    weight(2 * J, a_v, n2)
 
     c_x = load(4, x_h, n2)
     emit("kw")
@@ -658,6 +736,33 @@
     def stack(v):
         zero = jnp.zeros_like(v)
         return jnp.concatenate([jnp.where(lo, v, zero), jnp.where(lo, zero, v)], 0)
+
+    def row_parts(q):
+        rq = pl.ds(al(q * R), R)
+
+        def put(blk, more):
+            rr = pl.ds(al((q * S + blk) * R), R)
+            d = dg(kk[rr, :], wk[...], NT) + dg(vv[rr, :], wv[...], NT)
+            if more:
+                d += dg(dq_v[rq, :], wo[...], NT)
+            n = n1[rr, :].astype(f32)
+            sm[0:1, :] += jnp.sum(d * n, axis=0, keepdims=True)
+            sm[1:2, :] += jnp.sum(d, axis=0, keepdims=True)
+            dn[q % 2, blk // 2, blk % 2] = d.astype(bf16)
+
+        def others(i, _):
+            emit_when(
+                (f"d{qq}{ii}", (q == qq) & (i == ii))
+                for qq in range(C)
+                for ii in range(S - 1)
+                if qq + 1 < C or ii > 0
+            )
+            put((s + 1 + i) % S, False)
+            return 0
+
+        lax.fori_loop(0, S - 1, others, 0)
+        emit_when((f"d{qq}{S - 1}", q == qq) for qq in range(C))
+        put(s, True)
 
     def pair(t, _):
         q, p = t // pairs, t % pairs
@@ -672,49 +777,27 @@
         dl = jnp.sum(stack(dof * a_v[rq, lanes].astype(f32)), axis=1, keepdims=True)
         e_copy(t, slot).wait()
         dp = dg(dos, vv[rk, lanes], NT)
+        vv[rk, lanes] = dg(dos, e_v[slot], TN).astype(bf16).T
         ds = (e_v[slot].astype(f32) * (dp - dl)).astype(bf16)
+        dks = (dg(qs, ds, TN) * (1.0 / LOG2E)).astype(bf16).T
         dqs = dg(ds, kk[rk, lanes], NN)
+        kk[rk, lanes] = dks
         dq_v[rq, lanes] = (jnp.where(lo, dqs[:R], dqs[R:]) * (HEAD_DIM ** (-0.5))).astype(
             bf16
         )
-        kk[rk, lanes] = (dg(qs, ds, TN) * (1.0 / LOG2E)).astype(bf16).T
-        vv[rk, lanes] = dg(dos, e_v[slot], TN).astype(bf16).T
 
         @pl.when(t + 2 < C * pairs)
         def _():
             e_copy(t + 2, slot).start()
 
-        @pl.when(p == pairs - 1)
+        @pl.when((p == pairs - 1) & (q < C - 1))
         def _():
-            @pl.when(q == 2)
-            def _():
-                for i in range(4):
-                    dcp(0, i).wait_send()
-
-            def put(blk, more):
-                rr = pl.ds(al((q * S + blk) * R), R)
-                d = dg(kk[rr, :], wk[...], NT) + dg(vv[rr, :], wv[...], NT)
-                if more:
-                    d += dg(dq_v[rq, :], wo[...], NT)
-                n = n1[rr, :].astype(f32)
-                sm[0:1, :] += jnp.sum(d * n, axis=0, keepdims=True)
-                sm[1:2, :] += jnp.sum(d, axis=0, keepdims=True)
-                dn[q % 2, blk // 2, blk % 2] = d.astype(bf16)
-
-            def others(i, _):
-                emit_when(
-                    (f"d{qq}{ii}", (q == qq) & (i == ii)) for qq in range(C) for ii in range(S - 1)
-                )
-                put((s + 1 + i) % S, False)
-                return 0
-
-            lax.fori_loop(0, S - 1, others, 0)
-            emit_when((f"d{qq}{S - 1}", q == qq) for qq in range(C))
-            put(s, True)
+            row_parts(q)
 
         return 0
 
     lax.fori_loop(0, C * pairs, pair, 0)
+    emit("q")
     for u in (1, 2, 3):
         sent(u)
         cp5(u).wait_recv()
@@ -722,41 +805,29 @@
         r = pl.ds(i * R, R)
         a_v[r, :] = n1[pl.ds(al((i * S + s) * R), R), :]
     q_u, k_u, v_u = 2 * J + 1, 2 * J + 2, 2 * J + 3
-    emit("q")
-    gb[slot(q_u)] = dg(a_v[...], dq_v[...], TN).astype(bf16).reshape(B // 2, 2, CH, D)
+    weight(q_u, a_v, dq_v)
     sm[2:3, :] = jnp.sum(dq_v[...].astype(f32), axis=0, keepdims=True)
     sm[3:4, :] = jnp.sum(vv[0:t_rows, :].astype(f32), axis=0, keepdims=True)
-    sm[0:1, :] = (sm[0:1, :] - shift1 * sm[1:2, :]) / gain1
-
     def mcp(i, src, dst, dev):
         return remote(src, dst, ms.at[i], mr.at[i], dev)
 
+    emit("k")
+    weight(k_u, n1, kk.at[pl.ds(0, t_rows)])
+    h_rows, h_p = J // 2 * D, J // 2 * N
+    c_w0 = load(0, wd_h.at[pl.ds(0, h_rows)], kk.at[pl.ds(0, h_rows)])
+    emit("v")
+    weight(v_u, n1, vv.at[pl.ds(0, t_rows)])
+    c_p0 = load(1, p_h.at[pl.ds(0, h_p)], n1.at[pl.ds(0, h_p)])
+    emit("d20")
+    for i in range(4):
+        dcp(0, i).wait_send()
+    row_parts(C - 1)
+    sm[0:1, :] = (sm[0:1, :] - shift1 * sm[1:2, :]) / gain1
+
     m1 = mcp(0, sm, mc.at[0], (s, sib))
     m1.start()
-    emit("k")
-    for i in range(2):
-        gb[slot(k_u), 2 * i : 2 * i + 2] = (
-            dg(n1[:, i * (D // 2) : (i + 1) * (D // 2)], kk[0:t_rows, :], TN)
-            .astype(bf16)
-            .reshape(2, 2, CH, D)
-        )
-    m1.wait()
-    mz[0] = sm[...] + mc[0]
-    m2 = [mcp(k, mz.at[0], mz.at[k], (s, (z + k) % 4 * 2 + c)) for k in (1, 2, 3)]
-    for m in m2:
-        m.start()
-    c_wd = load(0, wd_h, kk)
-    emit("v")
-    for i in range(2):
-        gb[slot(v_u), 2 * i : 2 * i + 2] = (
-            dg(n1[:, i * (D // 2) : (i + 1) * (D // 2)], vv[0:t_rows, :], TN)
-            .astype(bf16)
-            .reshape(2, 2, CH, D)
-        )
-    c_p = load(1, p_h, n1)
-    emit("o0")
-    c_wd.wait()
-    c_p.wait()
+    c_w1 = load(2, wd_h.at[pl.ds(h_rows, h_rows)], kk.at[pl.ds(h_rows, h_rows)])
+    c_p1 = load(3, p_h.at[pl.ds(h_p, h_p)], n1.at[pl.ds(h_p, h_p)])
 
     def last(i):
         r = pl.ds(al(i * R), R)
@@ -765,29 +836,37 @@
             o += dg(n1[pl.ds(al(j * N + i * R), R), :], kk[j * D : (j + 1) * D, :], NN)
         q_v[r, :] = o.astype(bf16)
 
+    emit("o0")
+    for w in (c_w0, c_p0, c_w1, c_p1):
+        w.wait()
     last(0)
+    m1.wait()
+    mz[0] = sm[...] + mc[0]
+    m2 = [mcp(k, mz.at[0], mz.at[k], (s, (z + k) % 4 * 2 + c)) for k in (1, 2, 3)]
+    for m in m2:
+        m.start()
     emit("o1")
+    last(1)
     for m in m2:
         m.wait()
     mx[0] = (mz[0] + mz[1]) + (mz[2] + mz[3])
     m3 = mcp(4, mx.at[0], mx.at[1], (px, b))
     m3.start()
-    last(1)
     emit("o2")
+    last(2)
+    c_o = pltpu.make_async_copy(q_v, out_h, osem.at[0])
+    c_o.start()
     m3.wait()
     mx[2] = mx[0] + mx[1]
     m4 = mcp(5, mx.at[2], mx.at[3], (py, b))
     m4.start()
-    last(2)
-    c_o = pltpu.make_async_copy(q_v, out_h, osem.at[0])
-    c_o.start()
     emit("end0")
     m4.wait()
     sm[...] = mx[2] + mx[3]
     c_s = pltpu.make_async_copy(sm, sm_h, osem.at[2])
     c_s.start()
     emit("end1")
-    c_i = pltpu.make_async_copy(pb, ig_h, osem.at[1])
+    c_i = pltpu.make_async_copy(du, ig_h, osem.at[1])
     c_i.start()
     emit("end2")
     for u in range(U):
@@ -828,20 +907,20 @@
         out_specs=(ANY,) * 5,
         scratch_shapes=[
             vm((N, D), bf16), vm((N, D), bf16), vm((N, D), bf16),
-            vm((N, D), bf16), vm((N, D), bf16), vm((N, D), bf16),
+            vm((N, D), bf16), vm((N, D), bf16),
             vm((N, D), f32), vm((N, D), f32), vm((N, D), f32),
             vm((FF, D), bf16), vm((FF, D), bf16), vm((C * T, D), bf16),
             vm((D, D), bf16), vm((D, D), bf16), vm((D, D), bf16),
             vm((2 * J, 4, 2, CH, D), bf16), vm((2, 2, 2, R, D), bf16),
             vm((2, 2 * R, T), bf16), vm((16, D), f32),
-            vm((4, 4, CH, D), bf16), vm((2 * J, 4, CH // 2, D), bf16), vm((U, 3, CH // 2, D), bf16),
+            vm((5, 4, CH, D), bf16), vm((2 * J, 4, CH // 2, D), bf16), vm((U, 3, CH // 2, D), bf16),
             vm((4, CH // 2, D), bf16), vm((U, CH // 2, D), bf16), vm((U, CH, D), bf16),
-            vm((2, 2, 2, R // 2, D), bf16), vm((C, 2, R // 2, D), bf16),
+            vm((2, 2, 2, R // 2, D), bf16), vm((2, 2, R // 2, D), bf16),
             vm((1, 16, D), f32), vm((4, 16, D), f32), vm((4, 16, D), f32), vm((J, D), f32),
-            dma((4 + 2 * J + 4,)), dma((2,)), dma((4,)), dma((J,)),
+            dma((4 + 2 * J + 4,)), dma((2,)), dma((4,)), dma((J,)), dma((J,)), dma((J,)),
             dma((4, U)), dma((4, U)), dma((3, U)), dma((3, U)),
             dma((4, C)), dma((4, C)), dma((6,)), dma((6,)),
-            pltpu.SemaphoreType.REGULAR((4,)),
+            pltpu.SemaphoreType.REGULAR((5,)),
         ],
         compiler_params=pltpu.CompilerParams(
             collective_id=2, has_side_effects=True, vmem_limit_bytes=(64 * 2**20) - 2**17

time: 192 us -> 184 us (0.958)
  Pallas kernels: 191 us -> 183 us
    pallas_call x1, Pallas kernels: 55.4 us -> 49 us  [attend(): pl.pallas_call(functools.partial(attend_kernel, C, R, D, S), out_shape=(s...]
where the time goes in v4:
time: 184 us
  Pallas kernels  183 us (99%)
    pallas_call x1, Pallas kernels, backward(): pl.pallas_call(functools.partial(backward_kernel, C, R, D, S, FF), out_sh...  128 us
    pallas_call x1, Pallas kernels, attend(): pl.pallas_call(functools.partial(attend_kernel, C, R, D, S), out_shape=(s...  49 us
    pallas_call x1, Pallas kernels, finish(): pl.pallas_call(functools.partial(finish_kernel, D, FF), out_shape=(sd(out...  5.7 us

profile of v4, /device:TPU:0, one launch (start us, length us, event | category | flops | bytes accessed | tf_op | source)
XLA Modules:
  0.0 183.8 jit_solution(17979716695325341011)
XLA Ops:
  0.7 49.0 %shard_map.305 = (bf16[2688,768]{1,0:T(8,128)(2,1)}, bf16[672,768]{1,0:T(8,128)(2,1)}, bf16[2688,768]{1,0:T(8,128)(2,1)}, bf16[2688,768]{1,0:T(8,128)(2,1)}, bf1...) custom-call(bf16[672,768]{1,0:T(8,128)(2,1)} %bitcast.4, ...), custom_call_target="tpu_custom_call" | custom-call | flops 20000000000 | bytes 40000000 | tf_op jit(solution)/shard_map/pallas_call | solution.py:273
  49.7 128.2 %shard_map.306 = (bf16[672,768]{1,0:T(8,128)(2,1)}, bf16[672,768]{1,0:T(8,128)(2,1)}, bf16[12,96,768]{2,1,0:T(8,128)(2,1)}, f32[16,768]{1,0:T(8,128)}, bf16[2688,768]{1,0:T(8,128)(2,1)}) custom-call(bf16[672,768]{1,0:T(8,128)(2,1)} %bitcast.5, bf16[672,768]{1,0:T(8,128)(2,1)} %bitcast.7, bf16[672,768]{1,0:T(8,128)(2,1)} %get-tuple-element.46.a_h, ...), custom_call_target="tpu_custom_call" | custom-call | flops 40000000000 | bytes 60000000 | tf_op jit(solution)/shard_map/pallas_call | solution.py:897
  177.9 5.7 %shard_map.307 = (bf16[672,768]{1,0:T(8,128)(2,1)}, bf16[672,768]{1,0:T(8,128)(2,1)}, f32[96]{0:T(128)}, f32[96]{0:T(128)}, f32[96,768]{1,0:T(8,128)}, /*index=5...) custom-call(bf16[12,96,768]{2,1,0:T(8,128)(2,1)} %get-tuple-element., ...), custom_call_target="tpu_custom_call" | custom-call | tf_op jit(solution)/shard_map/pallas_call | solution.py:973

commit v5 on v4

--- a/solution.py
+++ b/solution.py
@@ -54,10 +54,10 @@
 
 def attend_kernel(
     C, R, D, S,
-    x_h, cot_h, len_s, g_r, s_r, bq_r, bv_r, wq_h, wk_h, wv_h, wd_h,
-    n1_h, q_h, k_h, v_h, a_h, li_h, e_h, gu_h,
-    x_v, n1, wq, wk, wv, q_v, k_v, v_v, a_v, li_v, e_v, s_v, cot, wd, gu,
-    lsem, osem, esem, gsem, os, orr, rs, rr,
+    x_h, cot_h, len_s, g_r, s_r, bq_r, bv_r, bo_r, g2_r, s2_r, wq_h, wk_h, wv_h, wd_h, wo_h,
+    n1_h, q_h, k_h, v_h, a_h, li_h, e_h, gu_h, h_h, n2_h,
+    x_v, n1, wq, wk, wv, q_v, k_v, v_v, a_v, li_v, e_v, s_v, cot, wd, gu, wo, h_v, n2,
+    lsem, osem, esem, gsem, rsem, os, orr, rs, rr,
 ):
     T = R * S
     HR = R // 2
@@ -76,7 +76,7 @@
         c.start()
     wc = [
         pltpu.make_async_copy(h, v, lsem.at[C + i])
-        for i, (h, v) in enumerate(((wk_h, wk), (wv_h, wv), (wq_h, wq), (cot_h, cot), (wd_h, wd)))
+        for i, (h, v) in enumerate(((wk_h, wk), (wv_h, wv), (wq_h, wq), (cot_h, cot), (wd_h, wd), (wo_h, wo)))
     ]
     for c in wc:
         c.start()
@@ -106,6 +106,7 @@
     ]
 
     gain, shift, bq, bv = (row(r) for r in (g_r, s_r, bq_r, bv_r))
+    b_out, gain2, shift2 = (row(r) for r in (bo_r, g2_r, s2_r))
     for q in range(C):
         xc[q].wait()
         z, _ = row_norm(x_v[q * R : (q + 1) * R, :].astype(f32))
@@ -213,6 +214,13 @@
         li_v[rq, lanes] = inv
         a_v[rq, lanes] = (jnp.where(lo, ol[:R], ol[R:]) * inv).astype(bf16)
 
+    def row_copies(q):
+        own_r = pl.ds(al(q * R), R)
+        return [
+            pltpu.make_async_copy(v.at[own_r], h.at[own_r], rsem.at[i, q])
+            for i, (v, h) in enumerate(((n2, n2_h), (a_v, a_h), (h_v, h_h), (li_v, li_h)))
+        ]
+
     def sequence(q, _):
         @pl.when(q == 1)
         def _():
@@ -243,13 +251,16 @@
             return 0
 
         lax.fori_loop(0, pairs // 2, two, 0)
+        own_r = pl.ds(al(q * R), R)
+        h = x_v[own_r, :].astype(f32) + dg(a_v[own_r, :], wo[...], NN) + b_out
+        h_v[own_r, :] = h
+        zn, _r = row_norm(h)
+        n2[own_r, :] = (zn * gain2 + shift2).astype(bf16)
+        for o in row_copies(q):
+            o.start()
         return 0
 
     lax.fori_loop(0, C, sequence, 0)
-    ac = pltpu.make_async_copy(a_v, a_h, osem.at[1])
-    lc = pltpu.make_async_copy(li_v, li_h, osem.at[2])
-    ac.start()
-    lc.start()
     e_copy(C * pairs - 2, 0).wait()
     e_copy(C * pairs - 1, 1).wait()
     for q in range(C):
@@ -262,11 +273,12 @@
     for j in range(J):
         gu_copy(j).wait()
     qc.wait()
-    ac.wait()
-    lc.wait()
-
-
-def attend(C, R, D, S, FF, x, cot, lengths, vecs, wq, wk, wv, wd):
+    for q in range(C):
+        for o in row_copies(q):
+            o.wait()
+
+
+def attend(C, R, D, S, FF, x, cot, lengths, vecs, wq, wk, wv, wd, wo):
     N, T, pairs = C * R, R * S, D // 128
     sd = jax.ShapeDtypeStruct
     dma = pltpu.SemaphoreType.DMA
@@ -281,9 +293,11 @@
             sd((N, D), f32),
             sd((C * pairs, 2 * R, T), bf16),
             sd((FF // D * N, D), bf16),
+            sd((N, D), f32),
+            sd((N, D), bf16),
         ),
-        in_specs=[ANY, ANY, SM] + [VM] * 4 + [ANY] * 4,
-        out_specs=(ANY,) * 8,
+        in_specs=[ANY, ANY, SM] + [VM] * 7 + [ANY] * 5,
+        out_specs=(ANY,) * 10,
         scratch_shapes=[
             pltpu.VMEM((N, D), bf16),
             pltpu.VMEM((C * T, D), bf16),
@@ -300,10 +314,14 @@
             pltpu.VMEM((N, D), bf16),
             pltpu.VMEM((FF, D), bf16),
             pltpu.VMEM((FF // D * N, D), bf16),
-            dma((C + 5,)),
-            dma((3 + 3 * C,)),
+            pltpu.VMEM((D, D), bf16),
+            pltpu.VMEM((N, D), f32),
+            pltpu.VMEM((N, D), bf16),
+            dma((C + 6,)),
+            dma((5 + 3 * C,)),
             dma((2,)),
             dma((FF // D,)),
+            dma((4, C)),
             dma((4, C)),
             dma((4, C)),
             dma((2, C)),
@@ -315,50 +333,46 @@
         cost_estimate=pl.CostEstimate(
             flops=20 * 10**9, bytes_accessed=40 * 10**6, transcendentals=0
         ),
-    )(x, cot, lengths, *vecs, wq, wk, wv, wd)
+    )(x, cot, lengths, *vecs, wq, wk, wv, wd, wo)
 
 
 SCHEDULE = {
-    "f11": ((1, 4),),
+    "f10": ((1, 4),),
     "f12": ((2, 0),),
-    "w1": ((2, 4),),
-    "f21": ((1, 5),),
-    "f22": ((2, 1),),
+    "u1": ((2, 4),),
+    "f22": ((2, 1), (1, 5),),
     "f30": ((3, 0),),
-    "u3": ((2, 2),),
-    "w3": ((2, 5),),
-    "s0": ((3, 1),),
-    "s1": ((2, 3),),
-    "s2": ((1, 6), (4, 0),),
-    "t0": ((2, 6), (3, 2),),
-    "t1": ((1, 7),),
-    "t3": ((4, 1),),
-    "t4": ((3, 3),),
-    "t5": ((2, 7),),
-    "d00": ((5, 1), (5, 0),),
-    "t6": ((6, 0), (10, 3), (10, 1), (10, 0), (10, 2), (3, 4),),
-    "t8": ((1, 8),),
-    "t11": ((4, 2), (2, 8),),
-    "d11": ((4, 4), (3, 5),),
-    "d12": ((4, 3), (7, 0),),
-    "t12": ((6, 1), (3, 6),),
-    "t16": ((5, 3),),
-    "q": ((5, 2),),
-    "k": ((1, 9), (3, 8), (4, 5), (4, 6), (3, 7), (2, 9),),
-    "v": ((1, 10), (7, 1),),
-    "d20": ((2, 10), (5, 6), (1, 11), (5, 4), (8, 0), (3, 9), (2, 11),),
-    "o0": ((6, 2), (3, 10),),
-    "o1": ((3, 11), (4, 8), (5, 5), (4, 7), (4, 10), (4, 9), (7, 2),),
-    "o2": ((5, 7), (8, 1), (4, 11), (5, 10), (5, 9), (5, 8),),
-    "end0": ((8, 2),),
-    "end2": ((5, 11),),
+    "f31": ((2, 5),),
+    "u3": ((2, 2), (1, 6),),
+    "s1": ((3, 1), (2, 6),),
+    "wo": ((2, 3), (4, 0), (1, 7),),
+    "t1": ((3, 2),),
+    "t2": ((2, 7),),
+    "d01": ((3, 3), (4, 1),),
+    "d02": ((5, 0),),
+    "t6": ((6, 0),),
+    "t8": ((10, 3), (10, 1), (1, 8), (10, 2), (4, 2), (10, 0), (3, 4), (3, 5), (5, 1),),
+    "t10": ((2, 8),),
+    "d10": ((3, 6),),
+    "d12": ((4, 3), (3, 7), (7, 0),),
+    "t12": ((5, 2), (4, 4), (6, 1),),
+    "t17": ((5, 3),),
+    "k": ((1, 9),),
+    "v": ((2, 9), (8, 0), (1, 10), (3, 8), (5, 4),),
+    "d20": ((4, 6), (1, 11), (2, 10), (4, 5), (2, 11),),
+    "d21": ((5, 6), (4, 7), (3, 9),),
+    "o0": ((6, 2), (5, 5), (4, 8), (3, 10), (4, 9), (3, 11),),
+    "o1": ((5, 7), (7, 1), (4, 10), (7, 2), (4, 11),),
+    "o2": ((5, 10), (5, 8), (5, 9),),
+    "end0": ((5, 11), (8, 1),),
+    "end1": ((8, 2),),
 }
 
 
 def backward_kernel(
     C, R, D, S, FF,
-    x_h, cot_h, a_h, li_h, q_h, k_h, v_h, n1_h, e_h, gu_h,
-    g1_r, s1_r, bo_r, g2_r, s2_r, bd_r, bu_r, wo_h, wu_h, wd_h, wq_h, wk_h, wv_h,
+    x_h, cot_h, a_h, li_h, q_h, k_h, v_h, n1_h, e_h, gu_h, h_h, n2_h,
+    g1_r, s1_r, g2_r, bd_r, bu_r, wo_h, wu_h, wd_h, wq_h, wk_h, wv_h,
     out_h, ig_h, f_h, sm_h, p_h,
     cot, a_v, q_v, n2, du, h_v, acc, dn2, kk, vv, n1, wk, wv, wo, gb, dn, e_v, sm,
     rc, r2, r3, s3, r4, f, d1, d2, mc, mz, mx, bup,
@@ -591,50 +605,39 @@
         cp.start()
         return cp
 
-    c_a = load(0, a_h, a_v)
-    c_wo = load(1, wo_h, wo)
-    c_x = load(2, x_h, du)
-    c_cot = load(3, cot_h, cot)
+    def tile(j):
+        return (
+            load(4 + 2 * j, wu_h.at[:, pl.ds(j * D, D)], vv.at[pl.ds(j * D, D)]),
+            load(5 + 2 * j, gu_h.at[pl.ds(j * N, N)], kk.at[pl.ds(j * N, N)]),
+        )
+
+    c_n2 = load(0, n2_h, n2)
+    c_w = [tile(0)]
+    c_cot = load(1, cot_h, cot)
+
     def e_copy(t, slot):
         return pltpu.make_async_copy(e_h.at[t], e_v.at[slot], esem.at[slot])
 
 
-    gain1, shift1, b_out, gain2, shift2, b_down = (
-        row(r) for r in (g1_r, s1_r, bo_r, g2_r, s2_r, bd_r)
-    )
+    gain1, shift1, gain2, b_down = (row(r) for r in (g1_r, s1_r, g2_r, bd_r))
     for j in range(J):
         bup[j : j + 1, :] = bu_r[j * D : (j + 1) * D].astype(f32).reshape(1, D)
     sm[...] = jnp.zeros_like(sm)
-    for w in (c_a, c_wo, c_x, c_cot):
-        w.wait()
-    c_w = [
-        (
-            load(4 + 2 * j, wu_h.at[:, pl.ds(j * D, D)], vv.at[pl.ds(j * D, D)]),
-            load(5 + 2 * j, gu_h.at[pl.ds(j * N, N)], kk.at[pl.ds(j * N, N)]),
-        )
-        for j in range(J)
-    ]
+    dn2[...] = jnp.zeros_like(dn2)
+    c_n2.wait()
+    c_w += [tile(j) for j in range(1, J)]
     n0 = 4 + 2 * J
+    c_a = load(0, a_h, a_v)
+    c_wo = load(2, wo_h, wo)
+    c_h = load(3, h_h, h_v)
     c_q = load(n0, q_h, q_v)
     c_n1 = load(n0 + 1, n1_h, n1)
     c_wk = load(n0 + 2, wk_h, wk)
     c_wv = load(n0 + 3, wv_h, wv)
     e_copy(0, 0).start()
     e_copy(1, 1).start()
-
-    def first(i, _):
-        r = pl.ds(al(i * R), R)
-        h = du[r, :].astype(f32) + dg(a_v[r, :], wo[...], NN) + b_out
-        h_v[r, :] = h
-        zn, _r = row_norm(h)
-        n2[r, :] = (zn * gain2 + shift2).astype(bf16)
-        acc[r, :] = h + b_down
-        dn2[r, :] = jnp.zeros((R, D), f32)
-        sm[7:8, :] += jnp.sum(cot[r, :].astype(f32), axis=0, keepdims=True)
-        return 0
-
-    lax.fori_loop(0, C, first, 0)
     pl.semaphore_wait(bar, len(beside))
+    c_cot.wait()
 
     def p_copy(j):
         return pltpu.make_async_copy(
@@ -694,13 +697,24 @@
 
     c_v = load(1, v_h, vv.at[pl.ds(0, t_rows)])
 
-    for j in range(J):
-        p_copy(j).wait()
-    c_k = load(0, k_h, kk.at[pl.ds(0, t_rows)])
+    for w in (c_a, c_wo, c_h):
+        w.wait()
+
+
+    c_k = pltpu.make_async_copy(k_h, kk.at[pl.ds(0, t_rows)], lsem.at[0])
 
     def second(i, _):
         emit_when((f"s{ii}", i == ii) for ii in range(C))
+
+        @pl.when(i == 1)
+        def _():
+            for j in range(J):
+                p_copy(j).wait()
+            c_k.start()
+
         r = pl.ds(al(i * R), R)
+        acc[r, :] = h_v[r, :] + b_down
+        sm[7:8, :] += jnp.sum(cot[r, :].astype(f32), axis=0, keepdims=True)
         zn, rr = row_norm(h_v[r, :])
         dnn = dn2[r, :]
         g = dnn * gain2
@@ -806,8 +820,6 @@
         a_v[r, :] = n1[pl.ds(al((i * S + s) * R), R), :]
     q_u, k_u, v_u = 2 * J + 1, 2 * J + 2, 2 * J + 3
     weight(q_u, a_v, dq_v)
-    sm[2:3, :] = jnp.sum(dq_v[...].astype(f32), axis=0, keepdims=True)
-    sm[3:4, :] = jnp.sum(vv[0:t_rows, :].astype(f32), axis=0, keepdims=True)
     def mcp(i, src, dst, dev):
         return remote(src, dst, ms.at[i], mr.at[i], dev)
 
@@ -822,6 +834,8 @@
     for i in range(4):
         dcp(0, i).wait_send()
     row_parts(C - 1)
+    sm[2:3, :] = jnp.sum(dq_v[...].astype(f32), axis=0, keepdims=True)
+    sm[3:4, :] = jnp.sum(vv[0:t_rows, :].astype(f32), axis=0, keepdims=True)
     sm[0:1, :] = (sm[0:1, :] - shift1 * sm[1:2, :]) / gain1
 
     m1 = mcp(0, sm, mc.at[0], (s, sib))
@@ -887,7 +901,7 @@
         o.wait()
 
 
-def backward(C, R, D, S, FF, x, cot, a, li, q, k, v, n1, e, gu, vecs, wo, wu, wd, wq, wk, wv):
+def backward(C, R, D, S, FF, x, cot, a, li, q, k, v, n1, e, gu, h, n2, vecs, wo, wu, wd, wq, wk, wv):
     N, T = C * R, R * S
     J = FF // D
     U, CH = 2 * J + 4, D // 8
@@ -903,7 +917,7 @@
             sd((16, D), f32),
             sd((J * N, D), bf16),
         ),
-        in_specs=[ANY] * 10 + [VM] * 7 + [ANY] * 6,
+        in_specs=[ANY] * 12 + [VM] * 5 + [ANY] * 6,
         out_specs=(ANY,) * 5,
         scratch_shapes=[
             vm((N, D), bf16), vm((N, D), bf16), vm((N, D), bf16),
@@ -928,42 +942,58 @@
         cost_estimate=pl.CostEstimate(
             flops=40 * 10**9, bytes_accessed=60 * 10**6, transcendentals=0
         ),
-    )(x, cot, a, li, q, k, v, n1, e, gu, *vecs, wo, wu, wd, wq, wk, wv)
+    )(x, cot, a, li, q, k, v, n1, e, gu, h, n2, *vecs, wo, wu, wd, wq, wk, wv)
 
 
 def finish_kernel(D, FF, f_h, sm, out_h, ig_h, *rest):
-    o_out, o_ig, g1, s1, wq, bq, wk, wv, bv, wo, bo, g2, s2, wu, bu, wd, bd, f, v_out, v_ig, sem = rest
+    (
+        o_out, o_ig, g1, s1, wq_o, bq, wk_o, wv_o, bv, wo_o, bo, g2, s2, wu_o, bu, wd_o, bd,
+        f, v_out, v_ig, up, low, sq, sem, osem,
+    ) = rest
     J, CH = FF // D, D // 8
-    c1 = pltpu.make_async_copy(f_h, f, sem.at[0])
-    c2 = pltpu.make_async_copy(out_h, v_out, sem.at[1])
-    c3 = pltpu.make_async_copy(ig_h, v_ig, sem.at[2])
-    for c in (c1, c2, c3):
+    parts = [
+        pltpu.make_async_copy(f_h.at[pl.ds(i * J, J)], f.at[pl.ds(i * J, J)], sem.at[i])
+        for i in range(3)
+    ]
+    c2 = pltpu.make_async_copy(out_h, v_out, sem.at[3])
+    c3 = pltpu.make_async_copy(ig_h, v_ig, sem.at[4])
+    for c in (*parts, c2, c3):
         c.start()
+    started = []
+
+    def write(v, o):
+        started.append(pltpu.make_async_copy(v, o, osem.at[len(started)]))
+        started[-1].start()
+
     b = lax.axis_index("batch")
-    c2.wait()
-    c4 = pltpu.make_async_copy(v_out, o_out, sem.at[1])
-    c4.start()
-    c3.wait()
-    c5 = pltpu.make_async_copy(v_ig, o_ig, sem.at[2])
-    c5.start()
     rolled = pltpu.roll(sm[0:8, :], (8 - b) % 8 * CH, 1)
     for i, o in enumerate((g1, s1, bq, bv, bo, g2, s2, bd)):
         o[...] = rolled[i, :CH]
     per = FF // 8
     half = D // per
-    up = sm[8 : 8 + J, :]
+    ub = sm[8 : 8 + J, :]
     here = lax.broadcasted_iota(jnp.int32, (J, 1), 0) == b // half
-    up = jnp.sum(jnp.where(here, up, 0.0), axis=0, keepdims=True)
-    up = jnp.where(b % half == 0, up[:, :per], up[:, per:])
-    bu[...] = up[0]
-    c1.wait()
+    ub = jnp.sum(jnp.where(here, ub, 0.0), axis=0, keepdims=True)
+    ub = jnp.where(b % half == 0, ub[:, :per], ub[:, per:])
+    bu[...] = ub[0]
+    parts[0].wait()
     for j in range(J):
-        wu[:, j * D : (j + 1) * D] = f[j].astype(f32)
-        wd[j * CH : (j + 1) * CH, :] = f[J + j].astype(f32)
-    for i, o in enumerate((wo, wq, wk, wv)):
-        o[...] = f[2 * J + i].astype(f32)
-    c4.wait()
-    c5.wait()
+        up[:, j * D : (j + 1) * D] = f[j].astype(f32)
+    write(up, wu_o)
+    parts[1].wait()
+    for j in range(J):
+        low[j * CH : (j + 1) * CH, :] = f[J + j].astype(f32)
+    write(low, wd_o)
+    parts[2].wait()
+    for i, o in enumerate((wo_o, wq_o, wk_o, wv_o)):
+        sq[i] = f[2 * J + i].astype(f32)
+        write(sq.at[i], o)
+    c2.wait()
+    write(v_out, o_out)
+    c3.wait()
+    write(v_ig, o_ig)
+    for c in started:
+        c.wait()
 
 
 def finish(D, FF, f, sm, out, ig):
@@ -977,8 +1007,10 @@
             row, row, row, sd((CH, FF), f32), sd((FF // 8,), f32), sd((FF // 8, D), f32), row,
         ),
         in_specs=[ANY, VM, ANY, ANY],
-        out_specs=(ANY, ANY) + (VM,) * 15,
-        scratch_shapes=[pltpu.VMEM(v.shape, bf16) for v in (f, out, ig)] + [pltpu.SemaphoreType.DMA((3,))],
+        out_specs=(ANY, ANY, VM, VM, ANY, VM, ANY, ANY, VM, ANY, VM, VM, VM, ANY, VM, ANY, VM),
+        scratch_shapes=[pltpu.VMEM(v.shape, bf16) for v in (f, out, ig)]
+        + [pltpu.VMEM((CH, FF), f32), pltpu.VMEM((FF // 8, D), f32), pltpu.VMEM((4, CH, D), f32)]
+        + [pltpu.SemaphoreType.DMA((5,)), pltpu.SemaphoreType.DMA((8,))],
         compiler_params=pltpu.CompilerParams(vmem_limit_bytes=62 * 2**20),
     )(f, sm, out, ig)
 
@@ -993,13 +1025,14 @@
     N = C * R
     x = inputs.reshape(N, D)
     cot = cotangent.reshape(N, D)
-    n1, q, k, v, a, li, e, gu = attend(
-        C, R, D, S, FF, x, cot, lengths, (gain_one, shift_one, b_query, b_value),
-        w_query, w_key, w_value, w_down,
+    n1, q, k, v, a, li, e, gu, h, n2 = attend(
+        C, R, D, S, FF, x, cot, lengths,
+        (gain_one, shift_one, b_query, b_value, b_out, gain_two, shift_two),
+        w_query, w_key, w_value, w_down, w_out,
     )
     out, input_grad, g, sm, _ = backward(
-        C, R, D, S, FF, x, cot, a, li, q, k, v, n1, e, gu,
-        (gain_one, shift_one, b_out, gain_two, shift_two, b_down, b_up),
+        C, R, D, S, FF, x, cot, a, li, q, k, v, n1, e, gu, h, n2,
+        (gain_one, shift_one, gain_two, b_down, b_up),
         w_out, w_up, w_down, w_query, w_key, w_value,
     )
     out, input_grad, *grads = finish(D, FF, g, sm, out, input_grad)

time: 184 us -> 178 us (0.967)
  Pallas kernels: 183 us -> 176 us
    pallas_call x1, Pallas kernels: 128 us -> 120 us  [backward(): pl.pallas_call(functools.partial(backward_kernel, C, R, D, S, FF), out_sh...]
    pallas_call x1, Pallas kernels: 49 us -> 50.9 us  [attend(): pl.pallas_call(functools.partial(attend_kernel, C, R, D, S), out_shape=(s...]
where the time goes in v5:
time: 178 us; the launch traced here: 177 us
  Pallas kernels  176 us (99%)
    pallas_call x1, Pallas kernels, backward(): pl.pallas_call(functools.partial(backward_kernel, C, R, D, S, FF), out_sh...  120 us
    pallas_call x1, Pallas kernels, attend(): pl.pallas_call(functools.partial(attend_kernel, C, R, D, S), out_shape=(s...  50.9 us
    pallas_call x1, Pallas kernels, finish(): pl.pallas_call(functools.partial(finish_kernel, D, FF), out_shape=(sd(out...  5.11 us

profile of v5, /device:TPU:0, one launch (start us, length us, event | category | flops | bytes accessed | tf_op | source)
XLA Modules:
  0.0 177.3 jit_solution(11600446392365654158)
XLA Ops:
  0.7 50.9 %shard_map.305 = (bf16[2688,768]{1,0:T(8,128)(2,1)}, bf16[672,768]{1,0:T(8,128)(2,1)}, bf16[2688,768]{1,0:T(8,128)(2,1)}, bf16[2688,768]{1,0:T(8,128)(2,1)}, bf1...) custom-call(bf16[672,768]{1,0:T(8,128)(2,1)} %bitcast.4, ...), custom_call_target="tpu_custom_call" | custom-call | flops 20000000000 | bytes 40000000 | tf_op jit(solution)/shard_map/pallas_call | solution.py:285
  51.5 120.5 %shard_map.306 = (bf16[672,768]{1,0:T(8,128)(2,1)}, bf16[672,768]{1,0:T(8,128)(2,1)}, bf16[12,96,768]{2,1,0:T(8,128)(2,1)}, f32[16,768]{1,0:T(8,128)}, bf16[2688,768]{1,0:T(8,128)(2,1)}) custom-call(bf16[672,768]{1,0:T(8,128)(2,1)} %bitcast.5, bf16[672,768]{1,0:T(8,128)(2,1)} %bitcast.7, bf16[672,768]{1,0:T(8,128)(2,1)} %get-tuple-element.48.a_h, ...), custom_call_target="tpu_custom_call" | custom-call | flops 40000000000 | bytes 60000000 | tf_op jit(solution)/shard_map/pallas_call | solution.py:911
  172.0 5.1 %shard_map.307 = (bf16[672,768]{1,0:T(8,128)(2,1)}, bf16[672,768]{1,0:T(8,128)(2,1)}, f32[96]{0:T(128)}, f32[96]{0:T(128)}, f32[96,768]{1,0:T(8,128)}, /*index=5...) custom-call(bf16[12,96,768]{2,1,0:T(8,128)(2,1)} %get-tuple-element., ...), custom_call_target="tpu_custom_call" | custom-call | tf_op jit(solution)/shard_map/pallas_call | solution.py:1003
